TPU v7x, 256 devices: a whole 4x4x8 slice. The times are simulated.
256 devices in a mesh: section: 16 (over z_hi, x, core), tp: 16 (over y, z_lo).
Axes of the slice: x: 4, y: 4, z: 8 (z_hi: 2, z_lo: 4; z = z_hi * 4 + z_lo), core: 2. Of those that a mesh axis runs over, the one named last changes fastest.
Arguments:
- query: bfloat16 [16, 2, 1024, 4096], P('section', None, 'tp'), may hold values from -6 to 6
- keys_values: bfloat16 [16, 2, 2, 1024, 512], P('section', None, None, 'tp'), may hold values from -6 to 6
- grad_out: bfloat16 [16, 2, 1024, 4096], P('section', None, 'tp'), may hold values from -6 to 6
- fwd_query: bfloat16 [16, 2, 1024, 4096], P('section', None, 'tp'), may hold values from -6 to 6
- fwd_keys_values: bfloat16 [16, 2, 2, 1024, 512], P('section', None, None, 'tp'), may hold values from -6 to 6
- held_out: bfloat16 [16, 2, 1024, 4096], P('section', None, None, 'tp'), may hold values from -4 to 4
- evict: int32 [8, 2, 2], replicated, may hold values from 0 to 1
Outputs:
- passed_on: bfloat16 [16, 2, 1024, 4096], P('section', None, 'tp')
- grad_query: bfloat16 [16, 2, 1024, 4096], P('section', None, 'tp')
- grad_keys_values: bfloat16 [16, 2, 2, 1024, 512], P('section', None, None, 'tp')
- mirror_out: bfloat16 [16, 2, 1024, 4096], P('section', None, None, 'tp')
All inputs are finite; a program needn't handle non-finite values.
Results may differ from a plain program's by a relative error of at most 0.0057.
Values may be sent and summed in bfloat16 or wider, within the bound.
No kernel may reach another device: no remote copies, remote signals or barrier semaphores. Data moves between devices by JAX's collectives and lax.ppermute only.
A program may use at most 128 MiB of HBM per device.

v0:
```python
import math

import jax
import jax.numpy as jnp
from jax import lax
from jax.sharding import PartitionSpec as P

HD = 128


def partner(value, axis, distance):
    mask = 2**distance
    pairs = [(source, source ^ mask) for source in range(lax.axis_size(axis))]
    return lax.ppermute(value, axis, pairs)


def shifted(block, axis, distance):
    devices = range(lax.axis_size(axis))
    route = [(i - distance, i) for i in devices if i - distance in devices]
    return lax.ppermute(block, axis, route)


def block_scores(q_block, keys, first):
    block_rows, width = q_block.shape
    head_dim = keys.shape[1]
    scale = 1.0 / math.sqrt(head_dim)
    q_heads = q_block.reshape(block_rows, width // head_dim, head_dim)
    scores = jnp.einsum("shd,td->hst", q_heads, keys, preferred_element_type=jnp.float32) * scale
    rows = first + jnp.arange(block_rows)[:, None]
    cols = jnp.arange(keys.shape[0])[None, :]
    scores = jnp.where((cols <= rows)[None], scores, -jnp.inf)
    top = jnp.max(scores, axis=2, keepdims=True)
    lse = top + jnp.log(jnp.sum(jnp.exp(scores - top), axis=2, keepdims=True))
    return (scores, lse, q_heads, scale)


def forward_pass(query, keys, values):
    seq, width = query.shape
    block_rows = seq // 8
    pieces = []
    for block in range(8):
        first = block * block_rows
        limit = first + block_rows
        scores, lse, q_heads, scale = block_scores(query[first:limit], keys[:limit], first)
        prob_b = jnp.exp(scores - lse).astype(jnp.bfloat16)
        out_b = jnp.einsum(
            "hst,td->shd", prob_b, values[:limit], preferred_element_type=jnp.float32
        )
        pieces.append(out_b.reshape(block_rows, width).astype(jnp.bfloat16))
    return jnp.concatenate(pieces, axis=0)


def backward_pass(query, keys, values, grad, held, flag):
    seq, width = query.shape
    head_dim = keys.shape[1]
    heads = width // head_dim
    block_rows = seq // 8
    dkeys = jnp.zeros((seq, head_dim), jnp.float32)
    dvalues = jnp.zeros((seq, head_dim), jnp.float32)
    dq_pieces = []
    for block in range(8):
        first = block * block_rows
        limit = first + block_rows
        scores, lse, q_heads, scale = block_scores(query[first:limit], keys[:limit], first)
        prob = jnp.exp(scores - lse)
        prob_b = prob.astype(jnp.bfloat16)
        out_b = jnp.einsum(
            "hst,td->shd", prob_b, values[:limit], preferred_element_type=jnp.float32
        )
        out_b = out_b.reshape(block_rows, width).astype(jnp.bfloat16)
        used = jnp.where(flag, held[first:limit], out_b)
        g_heads = grad[first:limit].reshape(block_rows, heads, head_dim)
        dprob = jnp.einsum(
            "shd,td->hst", g_heads, values[:limit], preferred_element_type=jnp.float32
        )
        delta = jnp.sum(
            g_heads.astype(jnp.float32)
            * used.reshape(block_rows, heads, head_dim).astype(jnp.float32),
            axis=2,
        ).T
        dscore = (prob * (dprob - delta[:, :, None])).astype(jnp.bfloat16)
        dquery = (
            jnp.einsum("hst,td->shd", dscore, keys[:limit], preferred_element_type=jnp.float32)
            * scale
        )
        dq_pieces.append(dquery.reshape(block_rows, width).astype(jnp.bfloat16))
        dkeys = dkeys.at[:limit].add(
            jnp.einsum("hst,shd->td", dscore, q_heads, preferred_element_type=jnp.float32) * scale
        )
        dvalues = dvalues.at[:limit].add(
            jnp.einsum("hst,shd->td", prob_b, g_heads, preferred_element_type=jnp.float32)
        )
    return (jnp.concatenate(dq_pieces, axis=0), dkeys, dvalues)


def per_device(query, keys_values, grad_out, fwd_query, fwd_keys_values, held_out, evict):
    query = query[0]
    keys_values = keys_values[0]
    grad_out = grad_out[0]
    fwd_query = fwd_query[0]
    fwd_keys_values = fwd_keys_values[0]
    held_local = held_out[0]
    sections = lax.axis_size("section")
    group_width = lax.axis_size("tp")
    section_pos = lax.axis_index("section")
    tp_pos = lax.axis_index("tp")
    micro = keys_values.shape[0]
    rows = keys_values.shape[2]
    kv_width = keys_values.shape[3]
    kv_count = kv_width // HD
    share = group_width // kv_count
    fwd_q, bwd_q, bwd_g = (
        lax.all_to_all(fwd_query, "tp", split_axis=2, concat_axis=1, tiled=True),
        lax.all_to_all(query, "tp", split_axis=2, concat_axis=1, tiled=True),
        lax.all_to_all(grad_out, "tp", split_axis=2, concat_axis=1, tiled=True),
    )
    fwd_all, bwd_all = (
        lax.all_gather(fwd_keys_values, "tp", axis=2, tiled=True),
        lax.all_gather(keys_values, "tp", axis=2, tiled=True),
    )
    fwd_kv = lax.dynamic_slice_in_dim(fwd_all, tp_pos // share * HD, HD, 3)
    bwd_kv = lax.dynamic_slice_in_dim(bwd_all, tp_pos // share * HD, HD, 3)
    outs = []
    for index in range(micro):
        outs.append(forward_pass(fwd_q[index], fwd_kv[index, 0], fwd_kv[index, 1]))
    stash_out = jnp.stack(outs)
    early = section_pos < sections // 2
    flag_pair = lax.dynamic_index_in_dim(
        evict, jnp.minimum(section_pos, sections // 2 - 1), 0, keepdims=False
    )
    fwd_marked = jnp.logical_and(early, flag_pair[0] == 1)
    bwd_marked = jnp.logical_and(early, flag_pair[1] == 1)
    sending = jnp.where(fwd_marked[:, None, None], stash_out, jnp.zeros_like(stash_out))
    bit_count = sections.bit_length() - 1
    kept_mirror = sending
    for bit in range(bit_count):
        kept_mirror = partner(kept_mirror, "section", bit)
    returned = held_local
    for bit in range(bit_count):
        returned = partner(returned, "section", bit)
    dqs = []
    dks = []
    dvs = []
    for index in range(micro):
        dquery, dkeys, dvalues = backward_pass(
            bwd_q[index],
            bwd_kv[index, 0],
            bwd_kv[index, 1],
            bwd_g[index],
            returned[index],
            bwd_marked[index],
        )
        dqs.append(dquery)
        dks.append(dkeys)
        dvs.append(dvalues)
    seq_out, seq_dq = (
        lax.all_to_all(stash_out, "tp", split_axis=1, concat_axis=2, tiled=True),
        lax.all_to_all(jnp.stack(dqs), "tp", split_axis=1, concat_axis=2, tiled=True),
    )
    partial_grads = jnp.stack([jnp.stack(dks), jnp.stack(dvs)], axis=1)
    grad_parts = lax.all_to_all(partial_grads, "tp", split_axis=2, concat_axis=3, tiled=True)
    grad_kv = jnp.sum(grad_parts.reshape(micro, 2, rows, kv_count, share, HD), axis=4)
    grad_kv = grad_kv.reshape(micro, 2, rows, kv_width).astype(jnp.bfloat16)
    passed = shifted(seq_out, "section", 1)
    return (passed[None], seq_dq[None], grad_kv[None], kept_mirror[None])


def solution(mesh):
    return jax.shard_map(
        per_device,
        mesh=mesh,
        in_specs=(
            P("section", None, "tp", None),
            P("section", None, None, "tp", None),
            P("section", None, "tp", None),
            P("section", None, "tp", None),
            P("section", None, None, "tp", None),
            P("section", None, None, "tp"),
            P(),
        ),
        out_specs=(
            P("section", None, "tp", None),
            P("section", None, "tp", None),
            P("section", None, None, "tp", None),
            P("section", None, None, "tp"),
        ),
        check_vma=False,
    )
```

profile of v0, /device:TPU:207, one launch (start us, length us, event | category | flops | bytes accessed | tf_op | source)
XLA Modules:
  0.0 609.4 jit_solution(11811173038006576100)
XLA Ops:
  7.9 5.5 copy.905
  13.4 3.2 bitcast_bitcast_fusion.1
  16.7 2.2 reshape.1900
  18.9 6.8 %all-to-all-start.2 = ((bf16[16,2,16384]{2,1,0:T(2,128)(2,1)}), bf16[16,2,16384]{2,1,0:T(2,128)(2,1)S(1)}, u32[]{:S(2)}, u32[]{:S(2)}) async-start(bf16[16,2,16384]{2,1,0:T(2,128)(2,1)} %reshape.1900), calls=%async_computation.2 | async-start | bytes 2097152 | tf_op jit(solution)/shard_map/all_to_all | solution.py:114
  28.3 3.8 copy.908
  32.1 3.2 bitcast_bitcast_fusion
  35.3 2.2 reshape.1898
  37.6 36.5 %all-to-all-done.2 = bf16[16,2,16384]{2,1,0:T(2,128)(2,1)S(1)} async-done(((bf16[16,2,16384]{2,1,0:T(2,128)(2,1)}), bf16[16,2,16384]{2,1,0:T(2,128)(2,1)S(1)}, u32[]{:S(2)}, u32[]{:S(2)}) %all-to-all-start.2) | async-done | bytes 1048608 | tf_op jit(solution)/shard_map/all_to_all | solution.py:114
  75.1 9.4 %all-to-all-start.3 = ((bf16[16,2,16384]{2,1,0:T(2,128)(2,1)}), bf16[16,2,16384]{2,1,0:T(2,128)(2,1)S(1)}, u32[]{:S(2)}, u32[]{:S(2)}) async-start(bf16[16,2,16384]{2,1,0:T(2,128)(2,1)} %reshape.1898), calls=%async_computation.3 | async-start | bytes 2097152 | tf_op jit(solution)/shard_map/all_to_all | solution.py:115
  85.2 4.0 copy.837
  89.2 3.2 bitcast_bitcast_fusion.2
  93.1 2.2 reshape.1896
  97.9 18.2 %collective-permute-done.2 = bf16[2,1024,256]{1,2,0:T(8,128)(2,1)} collective-permute-done((bf16[2,1024,256]{1,2,0:T(8,128)(2,1)}, bf16[2,1024,256]{1,2,0:T(8,128)(2,1)}, u32[]{:S(2)}, u32[]{:S(2)}) %collective-permute-start.2) | collective-permute-done | bytes 1048608 | tf_op jit(solution)/shard_map/ppermute | solution.py:14
  117.2 13.7 %all-to-all-done.3 = bf16[16,2,16384]{2,1,0:T(2,128)(2,1)S(1)} async-done(((bf16[16,2,16384]{2,1,0:T(2,128)(2,1)}), bf16[16,2,16384]{2,1,0:T(2,128)(2,1)S(1)}, u32[]{:S(2)}, u32[]{:S(2)}) %all-to-all-start.3) | async-done | bytes 1048608 | tf_op jit(solution)/shard_map/all_to_all | solution.py:115
  131.9 9.6 %all-to-all-start = ((bf16[16,2,16384]{2,1,0:T(2,128)(2,1)}), bf16[16,2,16384]{2,1,0:T(2,128)(2,1)S(1)}, u32[]{:S(2)}, u32[]{:S(2)}) async-start(bf16[16,2,16384]{2,1,0:T(2,128)(2,1)} %reshape.1896), calls=%async_computation | async-start | bytes 2097152 | tf_op jit(solution)/shard_map/all_to_all | solution.py:113
  147.2 5.0 reshape.1901
  152.2 3.5 copy.906
  158.4 5.0 reshape.1899
  163.5 3.5 copy.909
  188.4 31.6 %all-to-all-done = bf16[16,2,16384]{2,1,0:T(2,128)(2,1)S(1)} async-done(((bf16[16,2,16384]{2,1,0:T(2,128)(2,1)}), bf16[16,2,16384]{2,1,0:T(2,128)(2,1)S(1)}, u32[]{:S(2)}, u32[]{:S(2)}) %all-to-all-start) | async-done | bytes 1048608 | tf_op jit(solution)/shard_map/all_to_all | solution.py:113
  266.3 11.9 %fusion.192 = bf16[128,2,128]{2,0,1:T(8,128)(2,1)} fusion(bf16[2,128,896]{1,2,0:T(8,128)(2,1)S(1)} %fusion.39, bf16[2,2,1024,128]{3,2,1,0:T(8,128)(2,1)S(1)} %dynamic-slice_bitcast_fusion), kind=kOutput, calls=%fused_computation.285 | convolution fusion | flops 58785792 | bytes 753664 | tf_op jit(solution)/shard_map/hst,td->shd/dot_general | solution.py:83
  339.5 8.5 %all-to-all-start.4 = ((bf16[2,1024,256]{2,0,1:T(2,128)(2,1)}), bf16[2,1024,256]{2,0,1:T(2,128)(2,1)}, u32[]{:S(2)}, u32[]{:S(2)}) async-start(bf16[2,1024,256]{2,0,1:T(2,128)(2,1)} %copy.1038), calls=%async_computation.4 | async-start | bytes 2097152 | tf_op jit(solution)/shard_map/all_to_all | solution.py:158
  443.2 7.1 %all-to-all-start.1 = ((bf16[2,1024,256]{2,0,1:T(2,128)(2,1)}), bf16[2,1024,256]{2,0,1:T(2,128)(2,1)}, u32[]{:S(2)}, u32[]{:S(2)}) async-start(bf16[2,1024,256]{2,0,1:T(2,128)(2,1)} %copy.903), calls=%async_computation.1 | async-start | bytes 2097152 | tf_op jit(solution)/shard_map/all_to_all | solution.py:157
  455.9 2.9 copy.1073
  458.9 15.5 %all-to-all-done.1 = bf16[2,1024,256]{2,0,1:T(2,128)(2,1)} async-done(((bf16[2,1024,256]{2,0,1:T(2,128)(2,1)}), bf16[2,1024,256]{2,0,1:T(2,128)(2,1)}, u32[]{:S(2)}, u32[]{:S(2)}) %all-to-all-start.1) | async-done | bytes 1048608 | tf_op jit(solution)/shard_map/all_to_all | solution.py:157
  474.4 7.5 %all-to-all-start.5 = ((f32[2,2,1024,128]{3,0,1,2:T(2,128)}), f32[2,2,1024,128]{3,0,1,2:T(2,128)S(1)}, u32[]{:S(2)}, u32[]{:S(2)}) async-start(f32[2,2,1024,128]{3,0,1,2:T(2,128)} %copy.1073), calls=%async_computation.5 | async-start | bytes 4194304 | tf_op jit(solution)/shard_map/all_to_all | solution.py:161
  482.6 23.1 %collective-permute-done.6 = bf16[2,1024,256]{2,1,0:T(8,128)(2,1)} collective-permute-done((bf16[2,1024,256]{2,1,0:T(8,128)(2,1)}, bf16[2,1024,256]{2,1,0:T(8,128)(2,1)}, u32[]{:S(2)}, u32[]{:S(2)}) %collective-permute-start.6) | collective-permute-done | bytes 1048608 | tf_op jit(solution)/shard_map/ppermute | solution.py:14
  511.3 18.8 %collective-permute-done.7 = bf16[2,1024,256]{2,1,0:T(8,128)(2,1)} collective-permute-done((bf16[2,1024,256]{2,1,0:T(8,128)(2,1)}, bf16[2,1024,256]{2,1,0:T(8,128)(2,1)}, u32[]{:S(2)}, u32[]{:S(2)}) %collective-permute-start.7) | collective-permute-done | bytes 1048608 | tf_op jit(solution)/shard_map/ppermute | solution.py:14
  534.2 2.3 broadcast_in_dim.455
  538.9 58.6 %collective-permute-done.8 = bf16[2,1024,256]{2,1,0:T(8,128)(2,1)} collective-permute-done((bf16[2,1024,256]{2,1,0:T(8,128)(2,1)}, bf16[2,1024,256]{2,1,0:T(8,128)(2,1)}, u32[]{:S(2)}, u32[]{:S(2)}) %collective-permute-start.8) | collective-permute-done | bytes 1048608 | tf_op jit(solution)/shard_map/ppermute | solution.py:14
  597.6 2.3 copy.1437
  599.9 2.3 copy.1438
  (760 shorter events, 258.4 us)
Async XLA Ops:
  7.2 228.3 %all-gather.7.cloned.1.call-start = ((), (), s32[]{:S(2)}) async-start(), calls=%async_computation.7 | async-start | bytes 4456448 | tf_op jit(solution)/shard_map/all_gather | solution.py:119
  18.9 55.2 %all-to-all-start.2 = ((bf16[16,2,16384]{2,1,0:T(2,128)(2,1)}), bf16[16,2,16384]{2,1,0:T(2,128)(2,1)S(1)}, u32[]{:S(2)}, u32[]{:S(2)}) async-start(bf16[16,2,16384]{2,1,0:T(2,128)(2,1)} %reshape.1900), calls=%async_computation.2 | async-start | bytes 2097152 | tf_op jit(solution)/shard_map/all_to_all | solution.py:114
  27.0 65.4 %collective-permute-start.1 = (bf16[2,1024,256]{1,2,0:T(8,128)(2,1)}, bf16[2,1024,256]{1,2,0:T(8,128)(2,1)}, u32[]{:S(2)}, u32[]{:S(2)}) collective-permute-start(bf16[2,1024,256]{1,2,0:T(8,128)(2,1)} %bitcast.1303), channel_id=1, source_target_pairs={{0,16},{16,0},{32,48},{48,32},{64,80},{80,64},{96,112},{112,96},{1... | collective-permute-start | bytes 3145736 | tf_op jit(solution)/shard_map/ppermute | solution.py:14
  37.6 47.6 %copy-start.57 = (bf16[1,2,64,4096]{3,2,1,0:T(8,128)(2,1)S(1)}, bf16[1,2,64,4096]{3,2,1,0:T(8,128)(2,1)}, u32[]{:S(2)}) copy-start(bf16[1,2,64,4096]{3,2,1,0:T(8,128)(2,1)} %param.82) | copy-start | bytes 3145732
  75.1 55.8 %all-to-all-start.3 = ((bf16[16,2,16384]{2,1,0:T(2,128)(2,1)}), bf16[16,2,16384]{2,1,0:T(2,128)(2,1)S(1)}, u32[]{:S(2)}, u32[]{:S(2)}) async-start(bf16[16,2,16384]{2,1,0:T(2,128)(2,1)} %reshape.1898), calls=%async_computation.3 | async-start | bytes 2097152 | tf_op jit(solution)/shard_map/all_to_all | solution.py:115
  84.5 272.6 %all-gather.5.cloned.1.call-start = ((), (), s32[]{:S(2)}) async-start(), calls=%async_computation.6 | async-start | bytes 4456448 | tf_op jit(solution)/shard_map/all_gather | solution.py:118
  92.4 23.7 %collective-permute-start.2 = (bf16[2,1024,256]{1,2,0:T(8,128)(2,1)}, bf16[2,1024,256]{1,2,0:T(8,128)(2,1)}, u32[]{:S(2)}, u32[]{:S(2)}) collective-permute-start(bf16[2,1024,256]{1,2,0:T(8,128)(2,1)} %collective-permute-done.1), channel_id=1, source_target_pairs={{0,32},{16,48},{32,0},{48,16},{64,96},{80,112},{96,64},{112,80},{1... | collective-permute-start | bytes 3145736 | tf_op jit(solution)/shard_map/ppermute | solution.py:14
  116.1 28.8 %collective-permute-start.3 = (bf16[2,1024,256]{1,2,0:T(8,128)(2,1)}, bf16[2,1024,256]{1,2,0:T(8,128)(2,1)}, u32[]{:S(2)}, u32[]{:S(2)}) collective-permute-start(bf16[2,1024,256]{1,2,0:T(8,128)(2,1)} %collective-permute-done.2), channel_id=1, source_target_pairs={{0,64},{16,80},{32,96},{48,112},{64,0},{80,16},{96,32},{112,48},{1... | collective-permute-start | bytes 3145736 | tf_op jit(solution)/shard_map/ppermute | solution.py:14
  131.9 88.1 %all-to-all-start = ((bf16[16,2,16384]{2,1,0:T(2,128)(2,1)}), bf16[16,2,16384]{2,1,0:T(2,128)(2,1)S(1)}, u32[]{:S(2)}, u32[]{:S(2)}) async-start(bf16[16,2,16384]{2,1,0:T(2,128)(2,1)} %reshape.1896), calls=%async_computation | async-start | bytes 2097152 | tf_op jit(solution)/shard_map/all_to_all | solution.py:113
  144.9 88.5 %collective-permute-start.4 = (bf16[2,1024,256]{1,2,0:T(8,128)(2,1)}, bf16[2,1024,256]{1,2,0:T(8,128)(2,1)}, u32[]{:S(2)}, u32[]{:S(2)}) collective-permute-start(bf16[2,1024,256]{1,2,0:T(8,128)(2,1)} %collective-permute-done.3), channel_id=1, source_target_pairs={{0,128},{16,144},{32,160},{48,176},{64,192},{80,208},{96,224},{112... | collective-permute-start | bytes 3145736 | tf_op jit(solution)/shard_map/ppermute | solution.py:14
  168.6 70.0 %copy-start.80 = (bf16[128,2,128]{0,2,1:T(8,128)(2,1)}, bf16[128,2,128]{0,2,1:T(8,128)(2,1)S(1)}, u32[]{:S(2)}) copy-start(bf16[128,2,128]{0,2,1:T(8,128)(2,1)S(1)} %copy.911) | copy-start | bytes 196612
  168.7 71.0 %copy-start.84 = (bf16[128,2,128]{0,2,1:T(8,128)(2,1)}, bf16[128,2,128]{0,2,1:T(8,128)(2,1)S(1)}, u32[]{:S(2)}) copy-start(bf16[128,2,128]{0,2,1:T(8,128)(2,1)S(1)} %copy.919) | copy-start | bytes 196612
  238.9 41.7 %copy-start.91 = (f32[128,128]{1,0:T(8,128)}, f32[128,128]{1,0:T(8,128)S(1)}, u32[]{:S(2)}) copy-start(f32[128,128]{1,0:T(8,128)S(1)} %fusion.209) | copy-start | bytes 196612
  240.0 24.7 %copy-start.53 = (bf16[2,128,256]{1,2,0:T(8,128)(2,1)}, bf16[2,128,256]{1,2,0:T(8,128)(2,1)S(1)}, u32[]{:S(2)}) copy-start(bf16[2,128,256]{1,2,0:T(8,128)(2,1)S(1)} %fusion.146) | copy-start | bytes 393220
  242.2 21.6 %copy-start.50 = (bf16[2,128,384]{1,2,0:T(8,128)(2,1)}, bf16[2,128,384]{1,2,0:T(8,128)(2,1)S(1)}, u32[]{:S(2)}) copy-start(bf16[2,128,384]{1,2,0:T(8,128)(2,1)S(1)} %fusion.119) | copy-start | bytes 589828
  242.5 20.4 %copy-start.43 = (bf16[2,128,512]{1,2,0:T(8,128)(2,1)}, bf16[2,128,512]{1,2,0:T(8,128)(2,1)S(1)}, u32[]{:S(2)}) copy-start(bf16[2,128,512]{1,2,0:T(8,128)(2,1)S(1)} %fusion.85) | copy-start | bytes 786436
  245.0 17.0 %copy-start.39 = (bf16[2,128,640]{1,2,0:T(8,128)(2,1)}, bf16[2,128,640]{1,2,0:T(8,128)(2,1)S(1)}, u32[]{:S(2)}) copy-start(bf16[2,128,640]{1,2,0:T(8,128)(2,1)S(1)} %fusion.72) | copy-start | bytes 983044
  251.4 30.0 %copy-start.92 = (f32[128,128]{1,0:T(8,128)}, f32[128,128]{1,0:T(8,128)S(1)}, u32[]{:S(2)}) copy-start(f32[128,128]{1,0:T(8,128)S(1)} %fusion.208) | copy-start | bytes 196612
  251.8 28.3 %copy-start.17 = (f32[2,128,512]{1,2,0:T(8,128)}, f32[2,128,512]{1,2,0:T(8,128)S(1)}, u32[]{:S(2)}) copy-start(f32[2,128,512]{1,2,0:T(8,128)S(1)} %get-tuple-element.533) | copy-start | bytes 1572868
  255.8 23.3 %copy-start.41 = (bf16[2,128,640]{1,2,0:T(8,128)(2,1)}, bf16[2,128,640]{1,2,0:T(8,128)(2,1)S(1)}, u32[]{:S(2)}) copy-start(bf16[2,128,640]{1,2,0:T(8,128)(2,1)S(1)} %fusion.73) | copy-start | bytes 983044
  256.2 22.1 %copy-start.37 = (bf16[2,128,768]{1,2,0:T(8,128)(2,1)}, bf16[2,128,768]{1,2,0:T(8,128)(2,1)S(1)}, u32[]{:S(2)}) copy-start(bf16[2,128,768]{1,2,0:T(8,128)(2,1)S(1)} %fusion.53) | copy-start | bytes 1179652
  339.5 103.7 %all-to-all-start.4 = ((bf16[2,1024,256]{2,0,1:T(2,128)(2,1)}), bf16[2,1024,256]{2,0,1:T(2,128)(2,1)}, u32[]{:S(2)}, u32[]{:S(2)}) async-start(bf16[2,1024,256]{2,0,1:T(2,128)(2,1)} %copy.1038), calls=%async_computation.4 | async-start | bytes 2097152 | tf_op jit(solution)/shard_map/all_to_all | solution.py:158
  404.4 16.8 %copy-start.126 = (bf16[128,256]{1,0:T(8,128)(2,1)S(1)}, bf16[128,256]{1,0:T(8,128)(2,1)}, u32[]{:S(2)}) copy-start(bf16[128,256]{1,0:T(8,128)(2,1)} %copy.870) | copy-start | bytes 196612
  405.6 18.8 %copy-start.130 = (bf16[128,256]{1,0:T(8,128)(2,1)S(1)}, bf16[128,256]{1,0:T(8,128)(2,1)}, u32[]{:S(2)}) copy-start(bf16[128,256]{1,0:T(8,128)(2,1)} %copy.901) | copy-start | bytes 196612
  405.7 18.8 %copy-start.129 = (bf16[128,256]{1,0:T(8,128)(2,1)S(1)}, bf16[128,256]{1,0:T(8,128)(2,1)}, u32[]{:S(2)}) copy-start(bf16[128,256]{1,0:T(8,128)(2,1)} %copy.902) | copy-start | bytes 196612
  427.8 54.1 %collective-permute-start.5 = (bf16[2,1024,256]{2,1,0:T(8,128)(2,1)}, bf16[2,1024,256]{2,1,0:T(8,128)(2,1)}, u32[]{:S(2)}, u32[]{:S(2)}) collective-permute-start(bf16[2,1024,256]{2,1,0:T(8,128)(2,1)} %get-tuple-element.424), channel_id=1, source_target_pairs={{0,16},{16,0},{32,48},{48,32},{64,80},{80,64},{96,112},{112,96},{1... | collective-permute-start | bytes 3145736 | tf_op jit(solution)/shard_map/ppermute | solution.py:14
  443.2 31.2 %all-to-all-start.1 = ((bf16[2,1024,256]{2,0,1:T(2,128)(2,1)}), bf16[2,1024,256]{2,0,1:T(2,128)(2,1)}, u32[]{:S(2)}, u32[]{:S(2)}) async-start(bf16[2,1024,256]{2,0,1:T(2,128)(2,1)} %copy.903), calls=%async_computation.1 | async-start | bytes 2097152 | tf_op jit(solution)/shard_map/all_to_all | solution.py:157
  474.4 62.1 %all-to-all-start.5 = ((f32[2,2,1024,128]{3,0,1,2:T(2,128)}), f32[2,2,1024,128]{3,0,1,2:T(2,128)S(1)}, u32[]{:S(2)}, u32[]{:S(2)}) async-start(f32[2,2,1024,128]{3,0,1,2:T(2,128)} %copy.1073), calls=%async_computation.5 | async-start | bytes 4194304 | tf_op jit(solution)/shard_map/all_to_all | solution.py:161
  481.9 23.8 %collective-permute-start.6 = (bf16[2,1024,256]{2,1,0:T(8,128)(2,1)}, bf16[2,1024,256]{2,1,0:T(8,128)(2,1)}, u32[]{:S(2)}, u32[]{:S(2)}) collective-permute-start(bf16[2,1024,256]{2,1,0:T(8,128)(2,1)} %collective-permute-done.5), channel_id=1, source_target_pairs={{0,32},{16,48},{32,0},{48,16},{64,96},{80,112},{96,64},{112,80},{1... | collective-permute-start | bytes 3145736 | tf_op jit(solution)/shard_map/ppermute | solution.py:14
  505.7 24.3 %collective-permute-start.7 = (bf16[2,1024,256]{2,1,0:T(8,128)(2,1)}, bf16[2,1024,256]{2,1,0:T(8,128)(2,1)}, u32[]{:S(2)}, u32[]{:S(2)}) collective-permute-start(bf16[2,1024,256]{2,1,0:T(8,128)(2,1)} %collective-permute-done.6), channel_id=1, source_target_pairs={{0,64},{16,80},{32,96},{48,112},{64,0},{80,16},{96,32},{112,48},{1... | collective-permute-start | bytes 3145736 | tf_op jit(solution)/shard_map/ppermute | solution.py:14
  510.0 26.5 %collective-permute-start = (bf16[2,64,4096]{2,1,0:T(8,128)(2,1)}, bf16[2,64,4096]{2,1,0:T(8,128)(2,1)}, u32[]{:S(2)}, u32[]{:S(2)}) collective-permute-start(bf16[2,64,4096]{2,1,0:T(8,128)(2,1)} %all_to_all.74), channel_id=1, source_target_pairs={{0,16},{16,32},{32,48},{48,64},{64,80},{80,96},{96,112},{112,128},... | collective-permute-start | bytes 3145736 | tf_op jit(solution)/shard_map/ppermute | solution.py:20
  530.1 67.5 %collective-permute-start.8 = (bf16[2,1024,256]{2,1,0:T(8,128)(2,1)}, bf16[2,1024,256]{2,1,0:T(8,128)(2,1)}, u32[]{:S(2)}, u32[]{:S(2)}) collective-permute-start(bf16[2,1024,256]{2,1,0:T(8,128)(2,1)} %collective-permute-done.7), channel_id=1, source_target_pairs={{0,128},{16,144},{32,160},{48,176},{64,192},{80,208},{96,224},{112... | collective-permute-start | bytes 3145736 | tf_op jit(solution)/shard_map/ppermute | solution.py:14
  (168 other events, 651.8 us)
Sparse Core Ops, SparseCore 0:
  9.8 205.2 all-gather.6
  216.9 97.6 all-gather.4
where the time goes:
time: 621 us; the launch traced here: 609 us
  waiting for transfers between devices  217 us (35%)
  local copies, waits for them, and re-layouts  184 us (30%)
  matrix products  106 us (17%)
  starting transfers between devices  59 us (10%)
  other arithmetic  25 us (4%)
  between operations  17.6 us (3%)
    ppermute x8, waiting for transfers between devices, partner(): return lax.ppermute(value, axis, pairs)  119 us
    unnamed x409, local copies, waits for them, and re-layouts  77 us
    all_to_all x1, waiting for transfers between devices, per_device(): lax.all_to_all(query, 'tp', split_axis=2, concat_axis=1, tiled=True)  36.5 us
    all_to_all x1, waiting for transfers between devices, per_device(): lax.all_to_all(fwd_query, 'tp', split_axis=2, concat_axis=1, tiled=True)  31.6 us
    dot_general x16, matrix products, backward_pass(): jnp.einsum('hst,td->shd', dscore, keys[:limit], preferred_element_type=jn...  25.6 us
    dot_general x32, matrix products, block_scores(): jnp.einsum('shd,td->hst', q_heads, keys, preferred_element_type=jnp.float32)  25 us
    convert_element_type x16, local copies, waits for them, and re-layouts, backward_pass(): dq_pieces.append(dquery.reshape(block_rows, width).astype(jnp.bfloat16))  25 us
    reshape x32, local copies, waits for them, and re-layouts, block_scores(): q_heads = q_block.reshape(block_rows, width // head_dim, head_dim)  19.8 us
  transfers between devices with their start and end apart: 17, of which 8 were waited for; matrix products, arithmetic and copies ran while one was open for 50% of the time, Pallas kernels for 0%

commit v1 on v0

v1 whole, which is shorter than its diff:
```python
import math

import jax
import jax.numpy as jnp
from jax import lax
from jax.experimental import pallas as pl
from jax.experimental.pallas import tpu as pltpu
from jax.sharding import PartitionSpec as P

HD = 128
NY = 4
NZ = 4
ROWS = 64
WIDE = 1024
SUPER = 256
SCALE = 1.0 / math.sqrt(HD)
LOG2E = math.log2(math.e)
F32 = jnp.float32
BF16 = jnp.bfloat16

VMEM = pl.BlockSpec(memory_space=pltpu.VMEM)
SMEM = pl.BlockSpec(memory_space=pltpu.SMEM)


def call(body, outs, scratch=(), flops=0, nbytes=1 << 20, exps=0):
    def run(meta, *args):
        return pl.pallas_call(
            body,
            out_shape=[jax.ShapeDtypeStruct(s, d) for s, d in outs],
            in_specs=[SMEM] + [VMEM] * len(args),
            out_specs=[VMEM] * len(outs),
            scratch_shapes=list(scratch),
            compiler_params=pltpu.CompilerParams(vmem_limit_bytes=48 * 1024 * 1024),
            cost_estimate=pl.CostEstimate(
                flops=flops, bytes_accessed=nbytes, transcendentals=exps
            ),
        )(meta, *args)

    return run


def at(index, size):
    return pl.ds(pl.multiple_of(index * size, size), size)


def pack_kv_body(meta, fkv, bkv, *outs):
    y = meta[0]
    for k in range(NY):
        to = (y + k) % NY
        outs[k][0] = fkv[:, :, :, at(to, HD)]
        outs[k][1] = bkv[:, :, :, at(to, HD)]


def pack_one_body(meta, x, *outs):
    y = meta[0]
    for k in range(NY):
        outs[k][...] = x[:, :, at((y + k) % NY, WIDE)]


def pack_two_body(meta, a, b, *outs):
    y = meta[0]
    for k in range(NY):
        to = (y + k) % NY
        outs[k][0] = a[:, :, at(to, WIDE)]
        outs[k][1] = b[:, :, at(to, WIDE)]


def pack_held_body(meta, held, *outs):
    z = meta[1]
    for k in range(NZ):
        to = z ^ k
        for m in range(2):
            for yy in range(NY):
                outs[k][m, yy] = held[m, pl.ds(pl.multiple_of(yy * SUPER + to * ROWS, ROWS), ROWS), :]


def join_kv_body(meta, b0, b1, b2, b3, fwd, bwd):
    y = meta[0]
    for k, block in enumerate((b0, b1, b2, b3)):
        source = (y + NY - k) % NY
        fwd[source] = block[0]
        bwd[source] = block[1]


def join_wide_body(meta, b0, b1, b2, b3, out):
    y = meta[0]
    for k, block in enumerate((b0, b1, b2, b3)):
        out[:, :, at((y + NY - k) % NY, WIDE)] = block[...]


def join_mirror_body(meta, b0, b1, b2, b3, out):
    z = meta[1]
    for k, block in enumerate((b0, b1, b2, b3)):
        source = z ^ k
        for m in range(2):
            for yy in range(NY):
                out[m, pl.ds(pl.multiple_of(yy * SUPER + source * ROWS, ROWS), ROWS), :] = block[m, yy]


def reduce_kv_body(meta, own, b1, b2, b3, *outs):
    y = meta[0]
    for k in range(NY):
        to = (y + k) % NY
        total = own[to] + b1[to].astype(F32)
        total = total + (b2[to].astype(F32) + b3[to].astype(F32))
        outs[k][...] = total.astype(BF16)


def join_grad_kv_body(meta, b0, b1, b2, b3, out):
    y = meta[0]
    for k, block in enumerate((b0, b1, b2, b3)):
        out[:, :, :, at((y + NY - k) % NY, HD)] = block[...]


def load_heads(scratch, blocks, y, pick):
    for k, block in enumerate(blocks):
        source = (y + NY - k) % NY
        for m in range(2):
            for h in range(8):
                rows = slice((h % 4) * ROWS, (h % 4 + 1) * ROWS)
                cols = slice(h * HD, (h + 1) * HD)
                scratch[source, m, h // 4, rows, :] = pick(block, m, cols)


def load_keys(keys, values, blocks, z):
    for k, block in enumerate(blocks):
        source = z ^ k
        for m in range(2):
            for yy in range(NY):
                rows = pl.ds(pl.multiple_of(yy * SUPER + source * ROWS, ROWS), ROWS)
                keys[m, rows, :] = block[yy, m, 0]
                values[m, rows, :] = block[yy, m, 1]


def transposed(x):
    return x.astype(F32).T.astype(BF16)


def dot_nt(a, b):
    return lax.dot_general(a, b, (((1,), (1,)), ((), ())), preferred_element_type=F32)


def dot_nn(a, b):
    return lax.dot_general(a, b, (((1,), (0,)), ((), ())), preferred_element_type=F32)


def seen(z):
    key = lax.broadcasted_iota(jnp.int32, (SUPER, SUPER), 0)
    row = lax.broadcasted_iota(jnp.int32, (SUPER, SUPER), 1) % ROWS + z * ROWS
    return key <= row


def score_blocks(keys, m, q, stripe, mask):
    blocks = []
    for j in range(stripe + 1):
        s = dot_nt(keys[m, j * SUPER : (j + 1) * SUPER, :], q)
        if j == stripe:
            s = jnp.where(mask, s, -jnp.inf)
        blocks.append(s)
    top = blocks[0].max(axis=0, keepdims=True)
    for s in blocks[1:]:
        top = jnp.maximum(top, s.max(axis=0, keepdims=True))
    shift = top * (SCALE * LOG2E)
    exps = [jnp.exp2(s * (SCALE * LOG2E) - shift) for s in blocks]
    total = exps[0].sum(axis=0, keepdims=True)
    for e in exps[1:]:
        total = total + e.sum(axis=0, keepdims=True)
    return exps, 1.0 / total


def forward_body(meta, q0, q1, q2, q3, k0, k1, k2, k3, *rest):
    passes, mirrors = rest[:4], rest[4:8]
    qs, keys, values, values_t, outs = rest[8:]
    y, z = meta[0], meta[1]
    load_heads(qs, (q0, q1, q2, q3), y, lambda b, m, c: b[m, :, c])
    load_keys(keys, values, (k0, k1, k2, k3), z)
    for m in range(2):
        values_t[m] = transposed(values[m])
    mask = seen(z)

    @pl.loop(0, 4)
    def _(t):
        m, half = t // 2, t % 2
        for stripe in range(NY):
            exps, inverse = score_blocks(keys, m, qs[stripe, m, half], stripe, mask)
            out = jnp.zeros((HD, SUPER), F32)
            for j, e in enumerate(exps):
                out += dot_nn(values_t[m, :, j * SUPER : (j + 1) * SUPER], e.astype(BF16))
            outs[stripe, m, half] = (out * inverse).T.astype(BF16)

    for k in range(NY):
        to = (y + k) % NY
        for m in range(2):
            for h in range(8):
                rows = slice((h % 4) * ROWS, (h % 4 + 1) * ROWS)
                passes[k][m, :, h * HD : (h + 1) * HD] = outs[to, m, h // 4, rows, :]
    for k in range(NZ):
        to = z ^ k
        for m in range(2):
            sent = meta[2 + m] == 1
            for yy in range(NY):
                for e in range(2):
                    rows = pl.ds(pl.multiple_of((to % 2) * 128 + e * ROWS, ROWS), ROWS)
                    piece = outs[yy, m, to // 2, rows, :]
                    mirrors[k][m, yy, :, e * HD : (e + 1) * HD] = jnp.where(
                        sent, piece, jnp.zeros_like(piece)
                    )


def backward_body(meta, *rest):
    qg, kv, held = rest[:4], rest[4:8], rest[8:12]
    dqs, dkvs = rest[12:16], rest[16:20]
    qs, gs, hs, keys, values, keys_t, outs, dkeys, dvalues = rest[20:]
    y, z = meta[0], meta[1]
    load_heads(qs, qg, y, lambda b, m, c: b[0, m, :, c])
    load_heads(gs, qg, y, lambda b, m, c: b[1, m, :, c])
    load_keys(keys, values, kv, z)
    for k, block in enumerate(held):
        source = z ^ k
        for m in range(2):
            for yy in range(NY):
                for e in range(2):
                    rows = pl.ds(pl.multiple_of((source % 2) * 128 + e * ROWS, ROWS), ROWS)
                    hs[yy, m, source // 2, rows, :] = block[m, yy, :, e * HD : (e + 1) * HD]
    for m in range(2):
        keys_t[m] = transposed(keys[m])
    dkeys[...] = jnp.zeros_like(dkeys)
    dvalues[...] = jnp.zeros_like(dvalues)
    mask = seen(z)

    @pl.loop(0, 4)
    def _(t):
        m, half = t // 2, t % 2
        marked = meta[4 + m] == 1
        for stripe in range(NY):
            q, g = qs[stripe, m, half], gs[stripe, m, half]
            exps, inverse = score_blocks(keys, m, q, stripe, mask)
            kept = (g.astype(F32) * hs[stripe, m, half].astype(F32)).T
            kept = kept.sum(axis=0, keepdims=True)
            probs, dprobs = [], []
            delta = jnp.zeros((1, SUPER), F32)
            for j, e in enumerate(exps):
                p = e * inverse
                dp = dot_nt(values[m, j * SUPER : (j + 1) * SUPER, :], g)
                delta += (p * dp).sum(axis=0, keepdims=True)
                probs.append(p)
                dprobs.append(dp)
            delta = jnp.where(marked, kept, delta)
            dq = jnp.zeros((HD, SUPER), F32)
            for j, (p, dp) in enumerate(zip(probs, dprobs)):
                rows = slice(j * SUPER, (j + 1) * SUPER)
                ds = (p * (dp - delta)).astype(BF16)
                dq += dot_nn(keys_t[m, :, rows], ds)
                dkeys[m, rows, :] += dot_nn(ds, q)
                dvalues[m, rows, :] += dot_nn(p.astype(BF16), g)
            outs[stripe, m, half] = (dq * SCALE).T.astype(BF16)

    for k in range(NY):
        to = (y + k) % NY
        for m in range(2):
            for h in range(8):
                rows = slice((h % 4) * ROWS, (h % 4 + 1) * ROWS)
                dqs[k][m, :, h * HD : (h + 1) * HD] = outs[to, m, h // 4, rows, :]
    for k in range(NZ):
        to = z ^ k
        for m in range(2):
            for yy in range(NY):
                rows = pl.ds(pl.multiple_of(yy * SUPER + to * ROWS, ROWS), ROWS)
                dkvs[k][yy, m, 0] = (dkeys[m, rows, :] * SCALE).astype(dkvs[k].dtype)
                dkvs[k][yy, m, 1] = dvalues[m, rows, :].astype(dkvs[k].dtype)


def per_device(query, keys_values, grad_out, fwd_query, fwd_keys_values, held_out, evict):
    sections = lax.axis_size("section")
    half = sections // 2
    section = lax.axis_index("section")
    tp = lax.axis_index("tp")
    y, z = tp // NZ, tp % NZ
    flags = lax.dynamic_index_in_dim(evict, jnp.minimum(section, half - 1), 0, keepdims=False)
    flags = jnp.where(section < half, flags, 0)
    meta = jnp.concatenate([jnp.stack([y, z]).astype(jnp.int32), flags.reshape(4).astype(jnp.int32)])
    both = ("section", "tp")

    def index(s, yy, zz):
        return (s * NY + yy) * NZ + zz

    def along_y(x, k):
        pairs = [(yy * NZ + zz, (yy + k) % NY * NZ + zz) for yy in range(NY) for zz in range(NZ)]
        return lax.ppermute(x, "tp", pairs)

    def along_z(x, k):
        pairs = [(yy * NZ + zz, yy * NZ + (zz ^ k)) for yy in range(NY) for zz in range(NZ)]
        return lax.ppermute(x, "tp", pairs)

    def to_mirror(x, k, senders):
        pairs = [
            (index(s, yy, zz), index(sections - 1 - s, yy, zz ^ k))
            for s in senders
            for yy in range(NY)
            for zz in range(NZ)
        ]
        return lax.ppermute(x, both, pairs)

    def to_next(x, k):
        pairs = [
            (index(s, yy, zz), index(s + 1, (yy + k) % NY, zz))
            for s in range(sections - 1)
            for yy in range(NY)
            for zz in range(NZ)
        ]
        return lax.ppermute(x, both, pairs)

    kv_piece = ((2, 2, 2, ROWS, HD), BF16)
    kv_stripe = ((NY, 2, 2, ROWS, HD), BF16)
    wide = ((2, ROWS, WIDE), BF16)
    two_wide = ((2, 2, ROWS, WIDE), BF16)
    pair_piece = ((2, NY, ROWS, 2 * HD), BF16)
    heads = pltpu.VMEM((NY, 2, 2, SUPER, HD), BF16)
    whole = pltpu.VMEM((2, NZ * SUPER, HD), BF16)
    whole_t = pltpu.VMEM((2, HD, NZ * SUPER), BF16)
    total = pltpu.VMEM((2, NZ * SUPER, HD), F32)

    kv = call(pack_kv_body, [kv_piece] * NY)(meta, fwd_keys_values[0], keys_values[0])
    kv = [kv[0]] + [along_y(kv[k], k) for k in range(1, NY)]
    fq = call(pack_one_body, [wide] * NY, nbytes=2 << 20)(meta, fwd_query[0])
    fq = [fq[0]] + [along_y(fq[k], k) for k in range(1, NY)]
    fwd_kv, bwd_kv = call(join_kv_body, [kv_stripe] * 2)(meta, *kv)
    fwd_kv = [fwd_kv] + [along_z(fwd_kv, k) for k in range(1, NZ)]
    held = call(pack_held_body, [pair_piece] * NZ, nbytes=2 << 20)(meta, held_out[0])
    held = [to_mirror(held[k], k, range(half, sections)) for k in range(NZ)]
    qg = call(pack_two_body, [two_wide] * NY, nbytes=4 << 20)(meta, query[0], grad_out[0])
    qg = [qg[0]] + [along_y(qg[k], k) for k in range(1, NY)]
    bwd_kv = [bwd_kv] + [along_z(bwd_kv, k) for k in range(1, NZ)]

    pairs_done = 20 * 2 * 512 * 256
    fwd = call(
        forward_body,
        [wide] * NY + [pair_piece] * NZ,
        [heads, whole, whole, whole_t, heads],
        flops=4 * pairs_done * HD,
        nbytes=4 << 20,
        exps=pairs_done,
    )(meta, *fq, *fwd_kv)
    passed = [to_next(fwd[k], k) for k in range(NY)]
    mirror = [to_mirror(fwd[NY + k], k, range(half)) for k in range(NZ)]

    bwd = call(
        backward_body,
        [wide] * NY + [((NY, 2, 2, ROWS, HD), F32)] + [kv_stripe] * (NZ - 1),
        [heads, heads, heads, whole, whole, whole_t, heads, total, total],
        flops=10 * pairs_done * HD,
        nbytes=8 << 20,
        exps=pairs_done,
    )(meta, *qg, *bwd_kv, *held)
    dkv = [bwd[NY]] + [along_z(bwd[NY + k], k) for k in range(1, NZ)]
    dq = [bwd[0]] + [along_y(bwd[k], k) for k in range(1, NY)]
    dkv = call(reduce_kv_body, [((2, 2, ROWS, HD), BF16)] * NY)(meta, *dkv)
    dkv = [dkv[0]] + [along_y(dkv[k], k) for k in range(1, NY)]

    full = ((2, ROWS, NY * WIDE), BF16)
    (dq,) = call(join_wide_body, [full])(meta, *dq)
    (dkv,) = call(join_grad_kv_body, [((2, 2, ROWS, NY * HD), BF16)])(meta, *dkv)
    (passed,) = call(join_wide_body, [full])(meta, *passed)
    (mirror,) = call(join_mirror_body, [((2, NZ * SUPER, 2 * HD), BF16)])(meta, *mirror)
    return (passed[None], dq[None], dkv[None], mirror[None])


def solution(mesh):
    return jax.shard_map(
        per_device,
        mesh=mesh,
        in_specs=(
            P("section", None, "tp", None),
            P("section", None, None, "tp", None),
            P("section", None, "tp", None),
            P("section", None, "tp", None),
            P("section", None, None, "tp", None),
            P("section", None, None, "tp"),
            P(),
        ),
        out_specs=(
            P("section", None, "tp", None),
            P("section", None, "tp", None),
            P("section", None, None, "tp", None),
            P("section", None, None, "tp"),
        ),
        check_vma=False,
    )
```

time: 621 us -> 182 us (0.29)
  the two profiles are of different devices: /device:TPU:207 before, /device:TPU:224 now
where the time goes in v1:
time: 182 us
  starting transfers between devices  76.6 us (42%)
  waiting for transfers between devices  64.8 us (36%)
  Pallas kernels  33.9 us (19%)
  local copies, waits for them, and re-layouts  5.13 us (3%)
    ppermute x8, waiting for transfers between devices, to_mirror(): return lax.ppermute(x, both, pairs)  44.2 us
    pallas_call x12, Pallas kernels, run(): pl.pallas_call(body, out_shape=[jax.ShapeDtypeStruct(s, d) for s, d in ou...  33.9 us
    ppermute x15, starting transfers between devices, along_y(): return lax.ppermute(x, 'tp', pairs)  29.3 us
    ppermute x9, starting transfers between devices, along_z(): return lax.ppermute(x, 'tp', pairs)  21.3 us
    ppermute x8, starting transfers between devices, to_mirror(): return lax.ppermute(x, both, pairs)  13.7 us
    ppermute x9, waiting for transfers between devices, along_z(): return lax.ppermute(x, 'tp', pairs)  12.9 us
    ppermute x4, starting transfers between devices, to_next(): return lax.ppermute(x, both, pairs)  12.3 us
    ppermute x15, waiting for transfers between devices, along_y(): return lax.ppermute(x, 'tp', pairs)  7.76 us
  transfers between devices with their start and end apart: 36, of which 11 were waited for; matrix products, arithmetic and copies ran while one was open for 0% of the time, Pallas kernels for 18%

profile of v1, /device:TPU:224, one launch (start us, length us, event | category | flops | bytes accessed | tf_op | source)
XLA Modules:
  0.0 181.8 jit_solution(7399689554984415950)
XLA Ops:
  4.3 1.7 collective-permute-start.3
  5.9 2.9 %collective-permute-start.4 = (bf16[2,2,2,64,128]{4,3,2,1,0:T(8,128)(2,1)S(1)}, bf16[2,2,2,64,128]{4,3,2,1,0:T(8,128)(2,1)S(1)}, u32[]{:S(2)}, u32[]{:S(2)}) collective-permute-start(bf16[2,2,2,64,128]{4,3,2,1,0:T(8,128)(2,1)S(1)} %get-tuple-element.48), channel_id=1, source_target_pairs={{0,8},{1,9},{2,10},{3,11},{4,12},{5,13},{6,14},{7,15},{8,0},{9,1},... | collective-permute-start | bytes 393224 | tf_op jit(solution)/shard_map/ppermute | solution.py:289
  10.8 2.8 %collective-permute-start.1 = (bf16[2,64,1024]{2,1,0:T(8,128)(2,1)S(1)}, bf16[2,64,1024]{2,1,0:T(8,128)(2,1)S(1)}, u32[]{:S(2)}, u32[]{:S(2)}) collective-permute-start(bf16[2,64,1024]{2,1,0:T(8,128)(2,1)S(1)} %get-tuple-element.44), channel_id=1, source_target_pairs={{0,8},{1,9},{2,10},{3,11},{4,12},{5,13},{6,14},{7,15},{8,0},{9,1},... | collective-permute-start | bytes 786440 | tf_op jit(solution)/shard_map/ppermute | solution.py:289
  15.9 3.9 %collective-permute-start.19 = (bf16[2,4,64,256]{3,2,1,0:T(8,128)(2,1)S(1)}, bf16[2,4,64,256]{3,2,1,0:T(8,128)(2,1)S(1)}, u32[]{:S(2)}, u32[]{:S(2)}) collective-permute-start(bf16[2,4,64,256]{3,2,1,0:T(8,128)(2,1)S(1)} %get-tuple-element.60), channel_id=1, source_target_pairs={{128,112},{129,113},{130,114},{131,115},{132,116},{133,117},{134,1... | collective-permute-start | bytes 786440 | tf_op jit(solution)/shard_map/ppermute | solution.py:302
  20.8 7.7 %collective-permute-done.5.b3 = bf16[2,2,2,64,128]{4,3,2,1,0:T(8,128)(2,1)S(1)} collective-permute-done((bf16[2,2,2,64,128]{4,3,2,1,0:T(8,128)(2,1)S(1)}, bf16[2,2,2,64,128]{4,3,2,1,0:T(8,128)(2,1)S(1)}, u32[]{:S(2)}, u32[]{:S(2)}) %collective-permute-start.5) | collective-permute-done | bytes 131104 | tf_op jit(solution)/shard_map/ppermute | solution.py:289
  28.5 2.1 %collective-permute-start.20 = (bf16[2,4,64,256]{3,2,1,0:T(8,128)(2,1)S(1)}, bf16[2,4,64,256]{3,2,1,0:T(8,128)(2,1)S(1)}, u32[]{:S(2)}, u32[]{:S(2)}) collective-permute-start(bf16[2,4,64,256]{3,2,1,0:T(8,128)(2,1)S(1)} %get-tuple-element.61), channel_id=1, source_target_pairs={{128,113},{129,112},{130,115},{131,114},{132,117},{133,116},{134,1... | collective-permute-start | bytes 786440 | tf_op jit(solution)/shard_map/ppermute | solution.py:302
  33.9 2.0 %collective-permute-start.8 = (bf16[4,2,2,64,128]{4,3,2,1,0:T(8,128)(2,1)S(1)}, bf16[4,2,2,64,128]{4,3,2,1,0:T(8,128)(2,1)S(1)}, u32[]{:S(2)}, u32[]{:S(2)}) collective-permute-start(bf16[4,2,2,64,128]{4,3,2,1,0:T(8,128)(2,1)S(1)} %get-tuple-element.50.k0), channel_id=1, source_target_pairs={{0,3},{1,2},{2,1},{3,0},{4,7},{5,6},{6,5},{7,4},{8,11},{9,10},{10,... | collective-permute-start | bytes 786440 | tf_op jit(solution)/shard_map/ppermute | solution.py:293
  37.4 6.9 %collective-permute-done.20.rest_9_ = bf16[2,4,64,256]{3,2,1,0:T(8,128)(2,1)S(1)} collective-permute-done((bf16[2,4,64,256]{3,2,1,0:T(8,128)(2,1)S(1)}, bf16[2,4,64,256]{3,2,1,0:T(8,128)(2,1)S(1)}, u32[]{:S(2)}, u32[]{:S(2)}) %collective-permute-start.20) | collective-permute-done | bytes 262176 | tf_op jit(solution)/shard_map/ppermute | solution.py:302
  44.2 15.4 %collective-permute-done.21.rest_10_ = bf16[2,4,64,256]{3,2,1,0:T(8,128)(2,1)S(1)} collective-permute-done((bf16[2,4,64,256]{3,2,1,0:T(8,128)(2,1)S(1)}, bf16[2,4,64,256]{3,2,1,0:T(8,128)(2,1)S(1)}, u32[]{:S(2)}, u32[]{:S(2)}) %collective-permute-start.21) | collective-permute-done | bytes 262176 | tf_op jit(solution)/shard_map/ppermute | solution.py:302
  60.4 4.9 %collective-permute-done.22.rest_11_ = bf16[2,4,64,256]{3,2,1,0:T(8,128)(2,1)S(1)} collective-permute-done((bf16[2,4,64,256]{3,2,1,0:T(8,128)(2,1)S(1)}, bf16[2,4,64,256]{3,2,1,0:T(8,128)(2,1)S(1)}, u32[]{:S(2)}, u32[]{:S(2)}) %collective-permute-start.22) | collective-permute-done | bytes 262176 | tf_op jit(solution)/shard_map/ppermute | solution.py:302
  66.3 3.4 %collective-permute-start.14 = (bf16[2,2,64,1024]{3,2,1,0:T(8,128)(2,1)S(1)}, bf16[2,2,64,1024]{3,2,1,0:T(8,128)(2,1)S(1)}, u32[]{:S(2)}, u32[]{:S(2)}) collective-permute-start(bf16[2,2,64,1024]{3,2,1,0:T(8,128)(2,1)S(1)} %get-tuple-element.57), channel_id=1, source_target_pairs={{0,8},{1,9},{2,10},{3,11},{4,12},{5,13},{6,14},{7,15},{8,0},{9,1},... | collective-permute-start | bytes 1572872 | tf_op jit(solution)/shard_map/ppermute | solution.py:289
  70.0 2.1 %collective-permute-done.6.k1 = bf16[4,2,2,64,128]{4,3,2,1,0:T(8,128)(2,1)S(1)} collective-permute-done((bf16[4,2,2,64,128]{4,3,2,1,0:T(8,128)(2,1)S(1)}, bf16[4,2,2,64,128]{4,3,2,1,0:T(8,128)(2,1)S(1)}, u32[]{:S(2)}, u32[]{:S(2)}) %collective-permute-start.6) | collective-permute-done | bytes 262176 | tf_op jit(solution)/shard_map/ppermute | solution.py:293
  72.1 1.6 collective-permute-start.17
  73.8 2.5 %collective-permute-start.16 = (bf16[4,2,2,64,128]{4,3,2,1,0:T(8,128)(2,1)S(1)}, bf16[4,2,2,64,128]{4,3,2,1,0:T(8,128)(2,1)S(1)}, u32[]{:S(2)}, u32[]{:S(2)}) collective-permute-start(bf16[4,2,2,64,128]{4,3,2,1,0:T(8,128)(2,1)S(1)} %get-tuple-element.59.rest_4_), channel_id=1, source_target_pairs={{0,1},{1,0},{2,3},{3,2},{4,5},{5,4},{6,7},{7,6},{8,9},{9,8},{10,11... | collective-permute-start | bytes 786440 | tf_op jit(solution)/shard_map/ppermute | solution.py:293
  76.3 8.9 %shard_map.105 = (bf16[2,64,1024]{2,1,0:T(8,128)(2,1)S(1)}, bf16[2,64,1024]{2,1,0:T(8,128)(2,1)S(1)}, bf16[2,64,1024]{2,1,0:T(8,128)(2,1)S(1)}, bf16[2,64,1024]{...) custom-call(s32[6]{0:T(128)S(1)} %pad_add_fusion.meta, ...), custom_call_target="tpu_custom_call" | custom-call | flops 2684354560 | bytes 4194304 | tf_op jit(solution)/shard_map/pallas_call | solution.py:27
  85.2 2.0 %collective-permute-done.17.rest_6_ = bf16[4,2,2,64,128]{4,3,2,1,0:T(8,128)(2,1)S(1)} collective-permute-done((bf16[4,2,2,64,128]{4,3,2,1,0:T(8,128)(2,1)S(1)}, bf16[4,2,2,64,128]{4,3,2,1,0:T(8,128)(2,1)S(1)}, u32[]{:S(2)}, u32[]{:S(2)}) %collective-permute-start.17) | collective-permute-done | bytes 262176 | tf_op jit(solution)/shard_map/ppermute | solution.py:293
  87.2 1.9 %collective-permute-start.9 = (bf16[2,64,1024]{2,1,0:T(8,128)(2,1)S(1)}, bf16[2,64,1024]{2,1,0:T(8,128)(2,1)S(1)}, u32[]{:S(2)}, u32[]{:S(2)}) collective-permute-start(bf16[2,64,1024]{2,1,0:T(8,128)(2,1)S(1)} %get-tuple-element.51), channel_id=1, source_target_pairs={{0,16},{1,17},{2,18},{3,19},{4,20},{5,21},{6,22},{7,23},{8,24},{9,... | collective-permute-start | bytes 786440 | tf_op jit(solution)/shard_map/ppermute | solution.py:311
  89.1 3.0 %collective-permute-start.10 = (bf16[2,64,1024]{2,1,0:T(8,128)(2,1)S(1)}, bf16[2,64,1024]{2,1,0:T(8,128)(2,1)S(1)}, u32[]{:S(2)}, u32[]{:S(2)}) collective-permute-start(bf16[2,64,1024]{2,1,0:T(8,128)(2,1)S(1)} %get-tuple-element.52), channel_id=1, source_target_pairs={{0,20},{1,21},{2,22},{3,23},{4,24},{5,25},{6,26},{7,27},{8,28},{9,... | collective-permute-start | bytes 786440 | tf_op jit(solution)/shard_map/ppermute | solution.py:311
  92.1 4.5 %collective-permute-start.11 = (bf16[2,64,1024]{2,1,0:T(8,128)(2,1)S(1)}, bf16[2,64,1024]{2,1,0:T(8,128)(2,1)S(1)}, u32[]{:S(2)}, u32[]{:S(2)}) collective-permute-start(bf16[2,64,1024]{2,1,0:T(8,128)(2,1)S(1)} %get-tuple-element.53), channel_id=1, source_target_pairs={{0,24},{1,25},{2,26},{3,27},{4,28},{5,29},{6,30},{7,31},{8,16},{9,... | collective-permute-start | bytes 786440 | tf_op jit(solution)/shard_map/ppermute | solution.py:311
  96.7 2.9 %collective-permute-start.12 = (bf16[2,64,1024]{2,1,0:T(8,128)(2,1)S(1)}, bf16[2,64,1024]{2,1,0:T(8,128)(2,1)S(1)}, u32[]{:S(2)}, u32[]{:S(2)}) collective-permute-start(bf16[2,64,1024]{2,1,0:T(8,128)(2,1)S(1)} %get-tuple-element.54), channel_id=1, source_target_pairs={{0,28},{1,29},{2,30},{3,31},{4,16},{5,17},{6,18},{7,19},{8,20},{9,... | collective-permute-start | bytes 786440 | tf_op jit(solution)/shard_map/ppermute | solution.py:311
  100.9 15.2 %shard_map.109 = (bf16[2,64,1024]{2,1,0:T(8,128)(2,1)S(1)}, bf16[2,64,1024]{2,1,0:T(8,128)(2,1)S(1)}, bf16[2,64,1024]{2,1,0:T(8,128)(2,1)S(1)}, bf16[2,64,1024]{...) custom-call(s32[6]{0:T(128)S(1)} %pad_add_fusion.meta, ...), custom_call_target="tpu_custom_call" | custom-call | flops 6710886400 | bytes 8388608 | tf_op jit(solution)/shard_map/pallas_call | solution.py:27
  117.4 10.4 %collective-permute-start.26 = (bf16[4,2,2,64,128]{4,3,2,1,0:T(8,128)(2,1)S(1)}, bf16[4,2,2,64,128]{4,3,2,1,0:T(8,128)(2,1)S(1)}, u32[]{:S(2)}, u32[]{:S(2)}) collective-permute-start(bf16[4,2,2,64,128]{4,3,2,1,0:T(8,128)(2,1)S(1)} %get-tuple-element.69), channel_id=1, source_target_pairs={{0,1},{1,0},{2,3},{3,2},{4,5},{5,4},{6,7},{7,6},{8,9},{9,8},{10,11... | collective-permute-start | bytes 786440 | tf_op jit(solution)/shard_map/ppermute | solution.py:293
  127.9 1.9 %collective-permute-start.27 = (bf16[4,2,2,64,128]{4,3,2,1,0:T(8,128)(2,1)S(1)}, bf16[4,2,2,64,128]{4,3,2,1,0:T(8,128)(2,1)S(1)}, u32[]{:S(2)}, u32[]{:S(2)}) collective-permute-start(bf16[4,2,2,64,128]{4,3,2,1,0:T(8,128)(2,1)S(1)} %get-tuple-element.70), channel_id=1, source_target_pairs={{0,2},{1,3},{2,0},{3,1},{4,6},{5,7},{6,4},{7,5},{8,10},{9,11},{10,... | collective-permute-start | bytes 786440 | tf_op jit(solution)/shard_map/ppermute | solution.py:293
  133.7 4.2 %collective-permute-done.26.b1 = bf16[4,2,2,64,128]{4,3,2,1,0:T(8,128)(2,1)S(1)} collective-permute-done((bf16[4,2,2,64,128]{4,3,2,1,0:T(8,128)(2,1)S(1)}, bf16[4,2,2,64,128]{4,3,2,1,0:T(8,128)(2,1)S(1)}, u32[]{:S(2)}, u32[]{:S(2)}) %collective-permute-start.26) | collective-permute-done | bytes 262176 | tf_op jit(solution)/shard_map/ppermute | solution.py:293
  138.0 6.7 %collective-permute-start.23 = (bf16[2,64,1024]{2,1,0:T(8,128)(2,1)S(1)}, bf16[2,64,1024]{2,1,0:T(8,128)(2,1)S(1)}, u32[]{:S(2)}, u32[]{:S(2)}) collective-permute-start(bf16[2,64,1024]{2,1,0:T(8,128)(2,1)S(1)} %get-tuple-element.65), channel_id=1, source_target_pairs={{0,4},{1,5},{2,6},{3,7},{4,8},{5,9},{6,10},{7,11},{8,12},{9,13},{1... | collective-permute-start | bytes 786440 | tf_op jit(solution)/shard_map/ppermute | solution.py:289
  146.5 4.1 %collective-permute-done.28.b3 = bf16[4,2,2,64,128]{4,3,2,1,0:T(8,128)(2,1)S(1)} collective-permute-done((bf16[4,2,2,64,128]{4,3,2,1,0:T(8,128)(2,1)S(1)}, bf16[4,2,2,64,128]{4,3,2,1,0:T(8,128)(2,1)S(1)}, u32[]{:S(2)}, u32[]{:S(2)}) %collective-permute-start.28) | collective-permute-done | bytes 262176 | tf_op jit(solution)/shard_map/ppermute | solution.py:293
  151.4 9.9 %collective-permute-done.34.b2 = bf16[2,4,64,256]{3,2,1,0:T(8,128)(2,1)S(1)} collective-permute-done((bf16[2,4,64,256]{3,2,1,0:T(8,128)(2,1)S(1)}, bf16[2,4,64,256]{3,2,1,0:T(8,128)(2,1)S(1)}, u32[]{:S(2)}, u32[]{:S(2)}) %collective-permute-start.34) | collective-permute-done | bytes 262176 | tf_op jit(solution)/shard_map/ppermute | solution.py:302
  162.5 7.1 %collective-permute-done.35.b3 = bf16[2,4,64,256]{3,2,1,0:T(8,128)(2,1)S(1)} collective-permute-done((bf16[2,4,64,256]{3,2,1,0:T(8,128)(2,1)S(1)}, bf16[2,4,64,256]{3,2,1,0:T(8,128)(2,1)S(1)}, u32[]{:S(2)}, u32[]{:S(2)}) %collective-permute-start.35) | collective-permute-done | bytes 262176 | tf_op jit(solution)/shard_map/ppermute | solution.py:302
  169.6 2.9 %collective-permute-start.30 = (bf16[2,2,64,128]{3,2,1,0:T(8,128)(2,1)S(1)}, bf16[2,2,64,128]{3,2,1,0:T(8,128)(2,1)S(1)}, u32[]{:S(2)}, u32[]{:S(2)}) collective-permute-start(bf16[2,2,64,128]{3,2,1,0:T(8,128)(2,1)S(1)} %get-tuple-element.74), channel_id=1, source_target_pairs={{0,8},{1,9},{2,10},{3,11},{4,12},{5,13},{6,14},{7,15},{8,0},{9,1},... | collective-permute-start | bytes 196616 | tf_op jit(solution)/shard_map/ppermute | solution.py:289
  172.5 3.2 %collective-permute-start.31 = (bf16[2,2,64,128]{3,2,1,0:T(8,128)(2,1)S(1)}, bf16[2,2,64,128]{3,2,1,0:T(8,128)(2,1)S(1)}, u32[]{:S(2)}, u32[]{:S(2)}) collective-permute-start(bf16[2,2,64,128]{3,2,1,0:T(8,128)(2,1)S(1)} %get-tuple-element.75), channel_id=1, source_target_pairs={{0,12},{1,13},{2,14},{3,15},{4,0},{5,1},{6,2},{7,3},{8,4},{9,5},{1... | collective-permute-start | bytes 196616 | tf_op jit(solution)/shard_map/ppermute | solution.py:289
  175.7 1.6 shard_map.106
  178.9 1.6 shard_map.110
  (71 shorter events, 29.0 us)
Async XLA Ops:
  5.9 13.8 %collective-permute-start.4 = (bf16[2,2,2,64,128]{4,3,2,1,0:T(8,128)(2,1)S(1)}, bf16[2,2,2,64,128]{4,3,2,1,0:T(8,128)(2,1)S(1)}, u32[]{:S(2)}, u32[]{:S(2)}) collective-permute-start(bf16[2,2,2,64,128]{4,3,2,1,0:T(8,128)(2,1)S(1)} %get-tuple-element.48), channel_id=1, source_target_pairs={{0,8},{1,9},{2,10},{3,11},{4,12},{5,13},{6,14},{7,15},{8,0},{9,1},... | collective-permute-start | bytes 393224 | tf_op jit(solution)/shard_map/ppermute | solution.py:289
  10.7 19.9 %collective-permute-start = (bf16[2,64,1024]{2,1,0:T(8,128)(2,1)S(1)}, bf16[2,64,1024]{2,1,0:T(8,128)(2,1)S(1)}, u32[]{:S(2)}, u32[]{:S(2)}) collective-permute-start(bf16[2,64,1024]{2,1,0:T(8,128)(2,1)S(1)} %get-tuple-element.43), channel_id=1, source_target_pairs={{0,4},{1,5},{2,6},{3,7},{4,8},{5,9},{6,10},{7,11},{8,12},{9,13},{1... | collective-permute-start | bytes 786440 | tf_op jit(solution)/shard_map/ppermute | solution.py:289
  10.8 21.8 %collective-permute-start.1 = (bf16[2,64,1024]{2,1,0:T(8,128)(2,1)S(1)}, bf16[2,64,1024]{2,1,0:T(8,128)(2,1)S(1)}, u32[]{:S(2)}, u32[]{:S(2)}) collective-permute-start(bf16[2,64,1024]{2,1,0:T(8,128)(2,1)S(1)} %get-tuple-element.44), channel_id=1, source_target_pairs={{0,8},{1,9},{2,10},{3,11},{4,12},{5,13},{6,14},{7,15},{8,0},{9,1},... | collective-permute-start | bytes 786440 | tf_op jit(solution)/shard_map/ppermute | solution.py:289
  13.6 20.3 %collective-permute-start.2 = (bf16[2,64,1024]{2,1,0:T(8,128)(2,1)S(1)}, bf16[2,64,1024]{2,1,0:T(8,128)(2,1)S(1)}, u32[]{:S(2)}, u32[]{:S(2)}) collective-permute-start(bf16[2,64,1024]{2,1,0:T(8,128)(2,1)S(1)} %get-tuple-element.45), channel_id=1, source_target_pairs={{0,12},{1,13},{2,14},{3,15},{4,0},{5,1},{6,2},{7,3},{8,4},{9,5},{1... | collective-permute-start | bytes 786440 | tf_op jit(solution)/shard_map/ppermute | solution.py:289
  15.9 20.0 %collective-permute-start.19 = (bf16[2,4,64,256]{3,2,1,0:T(8,128)(2,1)S(1)}, bf16[2,4,64,256]{3,2,1,0:T(8,128)(2,1)S(1)}, u32[]{:S(2)}, u32[]{:S(2)}) collective-permute-start(bf16[2,4,64,256]{3,2,1,0:T(8,128)(2,1)S(1)} %get-tuple-element.60), channel_id=1, source_target_pairs={{128,112},{129,113},{130,114},{131,115},{132,116},{133,117},{134,1... | collective-permute-start | bytes 786440 | tf_op jit(solution)/shard_map/ppermute | solution.py:302
  28.5 15.7 %collective-permute-start.20 = (bf16[2,4,64,256]{3,2,1,0:T(8,128)(2,1)S(1)}, bf16[2,4,64,256]{3,2,1,0:T(8,128)(2,1)S(1)}, u32[]{:S(2)}, u32[]{:S(2)}) collective-permute-start(bf16[2,4,64,256]{3,2,1,0:T(8,128)(2,1)S(1)} %get-tuple-element.61), channel_id=1, source_target_pairs={{128,113},{129,112},{130,115},{131,114},{132,117},{133,116},{134,1... | collective-permute-start | bytes 786440 | tf_op jit(solution)/shard_map/ppermute | solution.py:302
  30.6 29.0 %collective-permute-start.21 = (bf16[2,4,64,256]{3,2,1,0:T(8,128)(2,1)S(1)}, bf16[2,4,64,256]{3,2,1,0:T(8,128)(2,1)S(1)}, u32[]{:S(2)}, u32[]{:S(2)}) collective-permute-start(bf16[2,4,64,256]{3,2,1,0:T(8,128)(2,1)S(1)} %get-tuple-element.62), channel_id=1, source_target_pairs={{128,114},{129,115},{130,112},{131,113},{132,118},{133,119},{134,1... | collective-permute-start | bytes 786440 | tf_op jit(solution)/shard_map/ppermute | solution.py:302
  32.6 32.7 %collective-permute-start.22 = (bf16[2,4,64,256]{3,2,1,0:T(8,128)(2,1)S(1)}, bf16[2,4,64,256]{3,2,1,0:T(8,128)(2,1)S(1)}, u32[]{:S(2)}, u32[]{:S(2)}) collective-permute-start(bf16[2,4,64,256]{3,2,1,0:T(8,128)(2,1)S(1)} %get-tuple-element.63), channel_id=1, source_target_pairs={{128,115},{129,114},{130,113},{131,112},{132,119},{133,118},{134,1... | collective-permute-start | bytes 786440 | tf_op jit(solution)/shard_map/ppermute | solution.py:302
  33.9 32.4 %collective-permute-start.8 = (bf16[4,2,2,64,128]{4,3,2,1,0:T(8,128)(2,1)S(1)}, bf16[4,2,2,64,128]{4,3,2,1,0:T(8,128)(2,1)S(1)}, u32[]{:S(2)}, u32[]{:S(2)}) collective-permute-start(bf16[4,2,2,64,128]{4,3,2,1,0:T(8,128)(2,1)S(1)} %get-tuple-element.50.k0), channel_id=1, source_target_pairs={{0,3},{1,2},{2,1},{3,0},{4,7},{5,6},{6,5},{7,4},{8,11},{9,10},{10,... | collective-permute-start | bytes 786440 | tf_op jit(solution)/shard_map/ppermute | solution.py:293
  35.9 33.8 %collective-permute-start.7 = (bf16[4,2,2,64,128]{4,3,2,1,0:T(8,128)(2,1)S(1)}, bf16[4,2,2,64,128]{4,3,2,1,0:T(8,128)(2,1)S(1)}, u32[]{:S(2)}, u32[]{:S(2)}) collective-permute-start(bf16[4,2,2,64,128]{4,3,2,1,0:T(8,128)(2,1)S(1)} %get-tuple-element.50.k0), channel_id=1, source_target_pairs={{0,2},{1,3},{2,0},{3,1},{4,6},{5,7},{6,4},{7,5},{8,10},{9,11},{10,... | collective-permute-start | bytes 786440 | tf_op jit(solution)/shard_map/ppermute | solution.py:293
  44.2 27.9 %collective-permute-start.6 = (bf16[4,2,2,64,128]{4,3,2,1,0:T(8,128)(2,1)S(1)}, bf16[4,2,2,64,128]{4,3,2,1,0:T(8,128)(2,1)S(1)}, u32[]{:S(2)}, u32[]{:S(2)}) collective-permute-start(bf16[4,2,2,64,128]{4,3,2,1,0:T(8,128)(2,1)S(1)} %get-tuple-element.50.k0), channel_id=1, source_target_pairs={{0,1},{1,0},{2,3},{3,2},{4,5},{5,4},{6,7},{7,6},{8,9},{9,8},{10,11... | collective-permute-start | bytes 786440 | tf_op jit(solution)/shard_map/ppermute | solution.py:293
  59.7 14.1 %collective-permute-start.18 = (bf16[4,2,2,64,128]{4,3,2,1,0:T(8,128)(2,1)S(1)}, bf16[4,2,2,64,128]{4,3,2,1,0:T(8,128)(2,1)S(1)}, u32[]{:S(2)}, u32[]{:S(2)}) collective-permute-start(bf16[4,2,2,64,128]{4,3,2,1,0:T(8,128)(2,1)S(1)} %get-tuple-element.59.rest_4_), channel_id=1, source_target_pairs={{0,3},{1,2},{2,1},{3,0},{4,7},{5,6},{6,5},{7,4},{8,11},{9,10},{10,... | collective-permute-start | bytes 786440 | tf_op jit(solution)/shard_map/ppermute | solution.py:293
  65.3 26.8 %collective-permute-start.13 = (bf16[2,2,64,1024]{3,2,1,0:T(8,128)(2,1)S(1)}, bf16[2,2,64,1024]{3,2,1,0:T(8,128)(2,1)S(1)}, u32[]{:S(2)}, u32[]{:S(2)}) collective-permute-start(bf16[2,2,64,1024]{3,2,1,0:T(8,128)(2,1)S(1)} %get-tuple-element.56), channel_id=1, source_target_pairs={{0,4},{1,5},{2,6},{3,7},{4,8},{5,9},{6,10},{7,11},{8,12},{9,13},{1... | collective-permute-start | bytes 1572872 | tf_op jit(solution)/shard_map/ppermute | solution.py:289
  66.3 30.3 %collective-permute-start.14 = (bf16[2,2,64,1024]{3,2,1,0:T(8,128)(2,1)S(1)}, bf16[2,2,64,1024]{3,2,1,0:T(8,128)(2,1)S(1)}, u32[]{:S(2)}, u32[]{:S(2)}) collective-permute-start(bf16[2,2,64,1024]{3,2,1,0:T(8,128)(2,1)S(1)} %get-tuple-element.57), channel_id=1, source_target_pairs={{0,8},{1,9},{2,10},{3,11},{4,12},{5,13},{6,14},{7,15},{8,0},{9,1},... | collective-permute-start | bytes 1572872 | tf_op jit(solution)/shard_map/ppermute | solution.py:289
  69.7 29.9 %collective-permute-start.15 = (bf16[2,2,64,1024]{3,2,1,0:T(8,128)(2,1)S(1)}, bf16[2,2,64,1024]{3,2,1,0:T(8,128)(2,1)S(1)}, u32[]{:S(2)}, u32[]{:S(2)}) collective-permute-start(bf16[2,2,64,1024]{3,2,1,0:T(8,128)(2,1)S(1)} %get-tuple-element.58), channel_id=1, source_target_pairs={{0,12},{1,13},{2,14},{3,15},{4,0},{5,1},{6,2},{7,3},{8,4},{9,5},{1... | collective-permute-start | bytes 1572872 | tf_op jit(solution)/shard_map/ppermute | solution.py:289
  72.1 15.0 %collective-permute-start.17 = (bf16[4,2,2,64,128]{4,3,2,1,0:T(8,128)(2,1)S(1)}, bf16[4,2,2,64,128]{4,3,2,1,0:T(8,128)(2,1)S(1)}, u32[]{:S(2)}, u32[]{:S(2)}) collective-permute-start(bf16[4,2,2,64,128]{4,3,2,1,0:T(8,128)(2,1)S(1)} %get-tuple-element.59.rest_4_), channel_id=1, source_target_pairs={{0,2},{1,3},{2,0},{3,1},{4,6},{5,7},{6,4},{7,5},{8,10},{9,11},{10,... | collective-permute-start | bytes 786440 | tf_op jit(solution)/shard_map/ppermute | solution.py:293
  73.8 15.3 %collective-permute-start.16 = (bf16[4,2,2,64,128]{4,3,2,1,0:T(8,128)(2,1)S(1)}, bf16[4,2,2,64,128]{4,3,2,1,0:T(8,128)(2,1)S(1)}, u32[]{:S(2)}, u32[]{:S(2)}) collective-permute-start(bf16[4,2,2,64,128]{4,3,2,1,0:T(8,128)(2,1)S(1)} %get-tuple-element.59.rest_4_), channel_id=1, source_target_pairs={{0,1},{1,0},{2,3},{3,2},{4,5},{5,4},{6,7},{7,6},{8,9},{9,8},{10,11... | collective-permute-start | bytes 786440 | tf_op jit(solution)/shard_map/ppermute | solution.py:293
  87.2 28.9 %collective-permute-start.9 = (bf16[2,64,1024]{2,1,0:T(8,128)(2,1)S(1)}, bf16[2,64,1024]{2,1,0:T(8,128)(2,1)S(1)}, u32[]{:S(2)}, u32[]{:S(2)}) collective-permute-start(bf16[2,64,1024]{2,1,0:T(8,128)(2,1)S(1)} %get-tuple-element.51), channel_id=1, source_target_pairs={{0,16},{1,17},{2,18},{3,19},{4,20},{5,21},{6,22},{7,23},{8,24},{9,... | collective-permute-start | bytes 786440 | tf_op jit(solution)/shard_map/ppermute | solution.py:311
  89.1 28.3 %collective-permute-start.10 = (bf16[2,64,1024]{2,1,0:T(8,128)(2,1)S(1)}, bf16[2,64,1024]{2,1,0:T(8,128)(2,1)S(1)}, u32[]{:S(2)}, u32[]{:S(2)}) collective-permute-start(bf16[2,64,1024]{2,1,0:T(8,128)(2,1)S(1)} %get-tuple-element.52), channel_id=1, source_target_pairs={{0,20},{1,21},{2,22},{3,23},{4,24},{5,25},{6,26},{7,27},{8,28},{9,... | collective-permute-start | bytes 786440 | tf_op jit(solution)/shard_map/ppermute | solution.py:311
  92.1 35.7 %collective-permute-start.11 = (bf16[2,64,1024]{2,1,0:T(8,128)(2,1)S(1)}, bf16[2,64,1024]{2,1,0:T(8,128)(2,1)S(1)}, u32[]{:S(2)}, u32[]{:S(2)}) collective-permute-start(bf16[2,64,1024]{2,1,0:T(8,128)(2,1)S(1)} %get-tuple-element.53), channel_id=1, source_target_pairs={{0,24},{1,25},{2,26},{3,27},{4,28},{5,29},{6,30},{7,31},{8,16},{9,... | collective-permute-start | bytes 786440 | tf_op jit(solution)/shard_map/ppermute | solution.py:311
  96.7 33.1 %collective-permute-start.12 = (bf16[2,64,1024]{2,1,0:T(8,128)(2,1)S(1)}, bf16[2,64,1024]{2,1,0:T(8,128)(2,1)S(1)}, u32[]{:S(2)}, u32[]{:S(2)}) collective-permute-start(bf16[2,64,1024]{2,1,0:T(8,128)(2,1)S(1)} %get-tuple-element.54), channel_id=1, source_target_pairs={{0,28},{1,29},{2,30},{3,31},{4,16},{5,17},{6,18},{7,19},{8,20},{9,... | collective-permute-start | bytes 786440 | tf_op jit(solution)/shard_map/ppermute | solution.py:311
  99.6 31.5 %collective-permute-start.32 = (bf16[2,4,64,256]{3,2,1,0:T(8,128)(2,1)S(1)}, bf16[2,4,64,256]{3,2,1,0:T(8,128)(2,1)S(1)}, u32[]{:S(2)}, u32[]{:S(2)}) collective-permute-start(bf16[2,4,64,256]{3,2,1,0:T(8,128)(2,1)S(1)} %get-tuple-element.76), channel_id=1, source_target_pairs={{0,240},{1,241},{2,242},{3,243},{4,244},{5,245},{6,246},{7,247},{8... | collective-permute-start | bytes 786440 | tf_op jit(solution)/shard_map/ppermute | solution.py:302
  116.1 16.3 %collective-permute-start.33 = (bf16[2,4,64,256]{3,2,1,0:T(8,128)(2,1)S(1)}, bf16[2,4,64,256]{3,2,1,0:T(8,128)(2,1)S(1)}, u32[]{:S(2)}, u32[]{:S(2)}) collective-permute-start(bf16[2,4,64,256]{3,2,1,0:T(8,128)(2,1)S(1)} %get-tuple-element.77), channel_id=1, source_target_pairs={{0,241},{1,240},{2,243},{3,242},{4,245},{5,244},{6,247},{7,246},{8... | collective-permute-start | bytes 786440 | tf_op jit(solution)/shard_map/ppermute | solution.py:302
  117.4 20.6 %collective-permute-start.26 = (bf16[4,2,2,64,128]{4,3,2,1,0:T(8,128)(2,1)S(1)}, bf16[4,2,2,64,128]{4,3,2,1,0:T(8,128)(2,1)S(1)}, u32[]{:S(2)}, u32[]{:S(2)}) collective-permute-start(bf16[4,2,2,64,128]{4,3,2,1,0:T(8,128)(2,1)S(1)} %get-tuple-element.69), channel_id=1, source_target_pairs={{0,1},{1,0},{2,3},{3,2},{4,5},{5,4},{6,7},{7,6},{8,9},{9,8},{10,11... | collective-permute-start | bytes 786440 | tf_op jit(solution)/shard_map/ppermute | solution.py:293
  127.9 17.2 %collective-permute-start.27 = (bf16[4,2,2,64,128]{4,3,2,1,0:T(8,128)(2,1)S(1)}, bf16[4,2,2,64,128]{4,3,2,1,0:T(8,128)(2,1)S(1)}, u32[]{:S(2)}, u32[]{:S(2)}) collective-permute-start(bf16[4,2,2,64,128]{4,3,2,1,0:T(8,128)(2,1)S(1)} %get-tuple-element.70), channel_id=1, source_target_pairs={{0,2},{1,3},{2,0},{3,1},{4,6},{5,7},{6,4},{7,5},{8,10},{9,11},{10,... | collective-permute-start | bytes 786440 | tf_op jit(solution)/shard_map/ppermute | solution.py:293
  129.7 20.8 %collective-permute-start.28 = (bf16[4,2,2,64,128]{4,3,2,1,0:T(8,128)(2,1)S(1)}, bf16[4,2,2,64,128]{4,3,2,1,0:T(8,128)(2,1)S(1)}, u32[]{:S(2)}, u32[]{:S(2)}) collective-permute-start(bf16[4,2,2,64,128]{4,3,2,1,0:T(8,128)(2,1)S(1)} %get-tuple-element.71), channel_id=1, source_target_pairs={{0,3},{1,2},{2,1},{3,0},{4,7},{5,6},{6,5},{7,4},{8,11},{9,10},{10,... | collective-permute-start | bytes 786440 | tf_op jit(solution)/shard_map/ppermute | solution.py:293
  131.1 30.2 %collective-permute-start.34 = (bf16[2,4,64,256]{3,2,1,0:T(8,128)(2,1)S(1)}, bf16[2,4,64,256]{3,2,1,0:T(8,128)(2,1)S(1)}, u32[]{:S(2)}, u32[]{:S(2)}) collective-permute-start(bf16[2,4,64,256]{3,2,1,0:T(8,128)(2,1)S(1)} %get-tuple-element.78), channel_id=1, source_target_pairs={{0,242},{1,243},{2,240},{3,241},{4,246},{5,247},{6,244},{7,245},{8... | collective-permute-start | bytes 786440 | tf_op jit(solution)/shard_map/ppermute | solution.py:302
  132.4 37.2 %collective-permute-start.35 = (bf16[2,4,64,256]{3,2,1,0:T(8,128)(2,1)S(1)}, bf16[2,4,64,256]{3,2,1,0:T(8,128)(2,1)S(1)}, u32[]{:S(2)}, u32[]{:S(2)}) collective-permute-start(bf16[2,4,64,256]{3,2,1,0:T(8,128)(2,1)S(1)} %get-tuple-element.79), channel_id=1, source_target_pairs={{0,243},{1,242},{2,241},{3,240},{4,247},{5,246},{6,245},{7,244},{8... | collective-permute-start | bytes 786440 | tf_op jit(solution)/shard_map/ppermute | solution.py:302
  138.0 34.5 %collective-permute-start.23 = (bf16[2,64,1024]{2,1,0:T(8,128)(2,1)S(1)}, bf16[2,64,1024]{2,1,0:T(8,128)(2,1)S(1)}, u32[]{:S(2)}, u32[]{:S(2)}) collective-permute-start(bf16[2,64,1024]{2,1,0:T(8,128)(2,1)S(1)} %get-tuple-element.65), channel_id=1, source_target_pairs={{0,4},{1,5},{2,6},{3,7},{4,8},{5,9},{6,10},{7,11},{8,12},{9,13},{1... | collective-permute-start | bytes 786440 | tf_op jit(solution)/shard_map/ppermute | solution.py:289
  145.1 33.8 %collective-permute-start.24 = (bf16[2,64,1024]{2,1,0:T(8,128)(2,1)S(1)}, bf16[2,64,1024]{2,1,0:T(8,128)(2,1)S(1)}, u32[]{:S(2)}, u32[]{:S(2)}) collective-permute-start(bf16[2,64,1024]{2,1,0:T(8,128)(2,1)S(1)} %get-tuple-element.66), channel_id=1, source_target_pairs={{0,8},{1,9},{2,10},{3,11},{4,12},{5,13},{6,14},{7,15},{8,0},{9,1},... | collective-permute-start | bytes 786440 | tf_op jit(solution)/shard_map/ppermute | solution.py:289
  150.5 28.3 %collective-permute-start.25 = (bf16[2,64,1024]{2,1,0:T(8,128)(2,1)S(1)}, bf16[2,64,1024]{2,1,0:T(8,128)(2,1)S(1)}, u32[]{:S(2)}, u32[]{:S(2)}) collective-permute-start(bf16[2,64,1024]{2,1,0:T(8,128)(2,1)S(1)} %get-tuple-element.67), channel_id=1, source_target_pairs={{0,12},{1,13},{2,14},{3,15},{4,0},{5,1},{6,2},{7,3},{8,4},{9,5},{1... | collective-permute-start | bytes 786440 | tf_op jit(solution)/shard_map/ppermute | solution.py:289
  161.3 19.2 %collective-permute-start.29 = (bf16[2,2,64,128]{3,2,1,0:T(8,128)(2,1)S(1)}, bf16[2,2,64,128]{3,2,1,0:T(8,128)(2,1)S(1)}, u32[]{:S(2)}, u32[]{:S(2)}) collective-permute-start(bf16[2,2,64,128]{3,2,1,0:T(8,128)(2,1)S(1)} %get-tuple-element.73), channel_id=1, source_target_pairs={{0,4},{1,5},{2,6},{3,7},{4,8},{5,9},{6,10},{7,11},{8,12},{9,13},{1... | collective-permute-start | bytes 196616 | tf_op jit(solution)/shard_map/ppermute | solution.py:289
  (12 other events, 144.2 us)

commit v2 on v1

--- a/solution.py
+++ b/solution.py
@@ -82,6 +82,12 @@
         bwd[source] = block[1]
 
 
+def pair_kv_body(meta, own, other, out):
+    z = meta[1]
+    out[z % 2] = own[...]
+    out[1 - z % 2] = other[...]
+
+
 def join_wide_body(meta, b0, b1, b2, b3, out):
     y = meta[0]
     for k, block in enumerate((b0, b1, b2, b3)):
@@ -122,7 +128,21 @@
                 scratch[source, m, h // 4, rows, :] = pick(block, m, cols)
 
 
-def load_keys(keys, values, blocks, z):
+def load_keys(keys, values, near, far_middle, far_end, z):
+    middle = jnp.logical_or(z == 1, z == 2)
+    for e in range(2):
+        for m in range(2):
+            for yy in range(NY):
+                rows = [
+                    pl.ds(pl.multiple_of(yy * SUPER + (pair * 2 + e) * ROWS, ROWS), ROWS)
+                    for pair in (z // 2, 1 - z // 2)
+                ]
+                for c, held in enumerate((keys, values)):
+                    held[m, rows[0], :] = near[e, yy, m, c]
+                    held[m, rows[1], :] = jnp.where(middle, far_middle[e, yy, m, c], far_end[e, yy, m, c])
+
+
+def load_keys_direct(keys, values, blocks, z):
     for k, block in enumerate(blocks):
         source = z ^ k
         for m in range(2):
@@ -173,7 +193,7 @@
     qs, keys, values, values_t, outs = rest[8:]
     y, z = meta[0], meta[1]
     load_heads(qs, (q0, q1, q2, q3), y, lambda b, m, c: b[m, :, c])
-    load_keys(keys, values, (k0, k1, k2, k3), z)
+    load_keys_direct(keys, values, (k0, k1, k2, k3), z)
     for m in range(2):
         values_t[m] = transposed(values[m])
     mask = seen(z)
@@ -208,13 +228,13 @@
 
 
 def backward_body(meta, *rest):
-    qg, kv, held = rest[:4], rest[4:8], rest[8:12]
-    dqs, dkvs = rest[12:16], rest[16:20]
-    qs, gs, hs, keys, values, keys_t, outs, dkeys, dvalues = rest[20:]
+    qg, kv, held = rest[:4], rest[4:7], rest[7:11]
+    dqs, dkvs = rest[11:15], rest[15:19]
+    qs, gs, hs, keys, values, keys_t, outs, dkeys, dvalues = rest[19:]
     y, z = meta[0], meta[1]
     load_heads(qs, qg, y, lambda b, m, c: b[0, m, :, c])
     load_heads(gs, qg, y, lambda b, m, c: b[1, m, :, c])
-    load_keys(keys, values, kv, z)
+    load_keys(keys, values, *kv, z)
     for k, block in enumerate(held):
         source = z ^ k
         for m in range(2):
@@ -310,6 +330,15 @@
         ]
         return lax.ppermute(x, both, pairs)
 
+    def spread_z(x):
+        swapped = along_z(x, 1)
+        (near,) = call(pair_kv_body, [kv_pair])(meta, x, swapped)
+        middle = [(yy * NZ + a, yy * NZ + b) for yy in range(NY) for a, b in ((1, 2), (2, 1))]
+        far_middle = lax.ppermute(near, "tp", middle)
+        ends = [(yy * NZ + a, yy * NZ + b) for yy in range(NY) for a, b in ((1, 0), (2, 3))]
+        return [near, far_middle, lax.ppermute(far_middle, "tp", ends)]
+
+    kv_pair = ((2, NY, 2, 2, ROWS, HD), BF16)
     kv_piece = ((2, 2, 2, ROWS, HD), BF16)
     kv_stripe = ((NY, 2, 2, ROWS, HD), BF16)
     wide = ((2, ROWS, WIDE), BF16)
@@ -330,7 +359,7 @@
     held = [to_mirror(held[k], k, range(half, sections)) for k in range(NZ)]
     qg = call(pack_two_body, [two_wide] * NY, nbytes=4 << 20)(meta, query[0], grad_out[0])
     qg = [qg[0]] + [along_y(qg[k], k) for k in range(1, NY)]
-    bwd_kv = [bwd_kv] + [along_z(bwd_kv, k) for k in range(1, NZ)]
+    bwd_kv = spread_z(bwd_kv)
 
     pairs_done = 20 * 2 * 512 * 256
     fwd = call(

time: 182 us -> 181 us (level); the launches traced: 182 us -> 178 us
  waiting for transfers between devices: 64.8 us -> 43.7 us
  starting transfers between devices: 76.6 us -> 95.9 us
  local copies, waits for them, and re-layouts: 5.13 us -> 2.02 us
    ppermute x8, waiting for transfers between devices: 44.2 us -> 17.5 us  [to_mirror(): return lax.ppermute(x, both, pairs)]
    ppermute x9 -> x7, starting transfers between devices: 21.3 us -> 39.2 us  [along_z(): return lax.ppermute(x, 'tp', pairs)]
    ppermute x9 -> x7, waiting for transfers between devices: 12.9 us -> 18 us  [along_z(): return lax.ppermute(x, 'tp', pairs)]
    ppermute x15, starting transfers between devices: 29.3 us -> 26.1 us  [along_y(): return lax.ppermute(x, 'tp', pairs)]
    unnamed x16, local copies, waits for them, and re-layouts: 5.05 us -> 1.94 us
    ppermute x0 -> x2, starting transfers between devices: none -> 1.98 us  [the longest x1 1.28 us: spread_z(): return [near, far_middle, lax.ppermute(far_middle, 'tp', ends)]]
    pallas_call x12 -> x13, Pallas kernels: 33.9 us -> 34.8 us  [run(): pl.pallas_call(body, out_shape=[jax.ShapeDtypeStruct(s, d) for s, d in ou...]
where the time goes in v2:
time: 181 us; the launch traced here: 178 us
  starting transfers between devices  95.9 us (53%)
  waiting for transfers between devices  43.7 us (24%)
  Pallas kernels  34.8 us (19%)
  local copies, waits for them, and re-layouts  2.02 us (1%)
    ppermute x7, starting transfers between devices, along_z(): return lax.ppermute(x, 'tp', pairs)  39.2 us
    pallas_call x13, Pallas kernels, run(): pl.pallas_call(body, out_shape=[jax.ShapeDtypeStruct(s, d) for s, d in ou...  34.8 us
    ppermute x15, starting transfers between devices, along_y(): return lax.ppermute(x, 'tp', pairs)  26.1 us
    ppermute x7, waiting for transfers between devices, along_z(): return lax.ppermute(x, 'tp', pairs)  18 us
    ppermute x8, waiting for transfers between devices, to_mirror(): return lax.ppermute(x, both, pairs)  17.5 us
    ppermute x8, starting transfers between devices, to_mirror(): return lax.ppermute(x, both, pairs)  14.8 us
    ppermute x4, starting transfers between devices, to_next(): return lax.ppermute(x, both, pairs)  13.9 us
    ppermute x15, waiting for transfers between devices, along_y(): return lax.ppermute(x, 'tp', pairs)  8.07 us
  transfers between devices with their start and end apart: 36, of which 11 were waited for; matrix products, arithmetic and copies ran while one was open for 0% of the time, Pallas kernels for 18%

profile of v2, /device:TPU:224, one launch (start us, length us, event | category | flops | bytes accessed | tf_op | source)
XLA Modules:
  0.0 178.4 jit_solution(15215500537734809689)
XLA Ops:
  4.4 1.7 collective-permute-start.3
  6.0 2.9 %collective-permute-start.4 = (bf16[2,2,2,64,128]{4,3,2,1,0:T(8,128)(2,1)S(1)}, bf16[2,2,2,64,128]{4,3,2,1,0:T(8,128)(2,1)S(1)}, u32[]{:S(2)}, u32[]{:S(2)}) collective-permute-start(bf16[2,2,2,64,128]{4,3,2,1,0:T(8,128)(2,1)S(1)} %get-tuple-element.48), channel_id=1, source_target_pairs={{0,8},{1,9},{2,10},{3,11},{4,12},{5,13},{6,14},{7,15},{8,0},{9,1},... | collective-permute-start | bytes 393224 | tf_op jit(solution)/shard_map/ppermute | solution.py:309
  11.0 4.0 %collective-permute-done.4.b2 = bf16[2,2,2,64,128]{4,3,2,1,0:T(8,128)(2,1)S(1)} collective-permute-done((bf16[2,2,2,64,128]{4,3,2,1,0:T(8,128)(2,1)S(1)}, bf16[2,2,2,64,128]{4,3,2,1,0:T(8,128)(2,1)S(1)}, u32[]{:S(2)}, u32[]{:S(2)}) %collective-permute-start.4) | collective-permute-done | bytes 131104 | tf_op jit(solution)/shard_map/ppermute | solution.py:309
  18.6 2.4 %collective-permute-start.1 = (bf16[2,64,1024]{2,1,0:T(8,128)(2,1)S(1)}, bf16[2,64,1024]{2,1,0:T(8,128)(2,1)S(1)}, u32[]{:S(2)}, u32[]{:S(2)}) collective-permute-start(bf16[2,64,1024]{2,1,0:T(8,128)(2,1)S(1)} %get-tuple-element.44), channel_id=1, source_target_pairs={{0,8},{1,9},{2,10},{3,11},{4,12},{5,13},{6,14},{7,15},{8,0},{9,1},... | collective-permute-start | bytes 786440 | tf_op jit(solution)/shard_map/ppermute | solution.py:309
  23.2 1.7 collective-permute-start.19
  26.9 2.1 %collective-permute-start.20 = (bf16[2,4,64,256]{3,2,1,0:T(8,128)(2,1)S(1)}, bf16[2,4,64,256]{3,2,1,0:T(8,128)(2,1)S(1)}, u32[]{:S(2)}, u32[]{:S(2)}) collective-permute-start(bf16[2,4,64,256]{3,2,1,0:T(8,128)(2,1)S(1)} %get-tuple-element.61), channel_id=1, source_target_pairs={{128,113},{129,112},{130,115},{131,114},{132,117},{133,116},{134,1... | collective-permute-start | bytes 786440 | tf_op jit(solution)/shard_map/ppermute | solution.py:322
  29.0 2.7 %collective-permute-done.1.q2 = bf16[2,64,1024]{2,1,0:T(8,128)(2,1)S(1)} collective-permute-done((bf16[2,64,1024]{2,1,0:T(8,128)(2,1)S(1)}, bf16[2,64,1024]{2,1,0:T(8,128)(2,1)S(1)}, u32[]{:S(2)}, u32[]{:S(2)}) %collective-permute-start.1) | collective-permute-done | bytes 262176 | tf_op jit(solution)/shard_map/ppermute | solution.py:309
  33.1 3.0 %collective-permute-start.8 = (bf16[4,2,2,64,128]{4,3,2,1,0:T(8,128)(2,1)S(1)}, bf16[4,2,2,64,128]{4,3,2,1,0:T(8,128)(2,1)S(1)}, u32[]{:S(2)}, u32[]{:S(2)}) collective-permute-start(bf16[4,2,2,64,128]{4,3,2,1,0:T(8,128)(2,1)S(1)} %get-tuple-element.50.k0), channel_id=1, source_target_pairs={{0,3},{1,2},{2,1},{3,0},{4,7},{5,6},{6,5},{7,4},{8,11},{9,10},{10,... | collective-permute-start | bytes 786440 | tf_op jit(solution)/shard_map/ppermute | solution.py:313
  37.3 5.8 %collective-permute-done.20.rest_8_ = bf16[2,4,64,256]{3,2,1,0:T(8,128)(2,1)S(1)} collective-permute-done((bf16[2,4,64,256]{3,2,1,0:T(8,128)(2,1)S(1)}, bf16[2,4,64,256]{3,2,1,0:T(8,128)(2,1)S(1)}, u32[]{:S(2)}, u32[]{:S(2)}) %collective-permute-start.20) | collective-permute-done | bytes 262176 | tf_op jit(solution)/shard_map/ppermute | solution.py:322
  43.1 18.0 %collective-permute-start.6 = (bf16[4,2,2,64,128]{4,3,2,1,0:T(8,128)(2,1)S(1)}, bf16[4,2,2,64,128]{4,3,2,1,0:T(8,128)(2,1)S(1)}, u32[]{:S(2)}, u32[]{:S(2)}) collective-permute-start(bf16[4,2,2,64,128]{4,3,2,1,0:T(8,128)(2,1)S(1)} %get-tuple-element.50.k0), channel_id=1, source_target_pairs={{0,1},{1,0},{2,3},{3,2},{4,5},{5,4},{6,7},{7,6},{8,9},{9,8},{10,11... | collective-permute-start | bytes 786440 | tf_op jit(solution)/shard_map/ppermute | solution.py:313
  64.1 8.0 %collective-permute-done.7.k2 = bf16[4,2,2,64,128]{4,3,2,1,0:T(8,128)(2,1)S(1)} collective-permute-done((bf16[4,2,2,64,128]{4,3,2,1,0:T(8,128)(2,1)S(1)}, bf16[4,2,2,64,128]{4,3,2,1,0:T(8,128)(2,1)S(1)}, u32[]{:S(2)}, u32[]{:S(2)}) %collective-permute-start.7) | collective-permute-done | bytes 262176 | tf_op jit(solution)/shard_map/ppermute | solution.py:313
  73.6 4.5 %collective-permute-start.22 = (bf16[2,4,64,256]{3,2,1,0:T(8,128)(2,1)S(1)}, bf16[2,4,64,256]{3,2,1,0:T(8,128)(2,1)S(1)}, u32[]{:S(2)}, u32[]{:S(2)}) collective-permute-start(bf16[2,4,64,256]{3,2,1,0:T(8,128)(2,1)S(1)} %get-tuple-element.63), channel_id=1, source_target_pairs={{128,115},{129,114},{130,113},{131,112},{132,119},{133,118},{134,1... | collective-permute-start | bytes 786440 | tf_op jit(solution)/shard_map/ppermute | solution.py:322
  78.1 8.9 %shard_map.105 = (bf16[2,64,1024]{2,1,0:T(8,128)(2,1)S(1)}, bf16[2,64,1024]{2,1,0:T(8,128)(2,1)S(1)}, bf16[2,64,1024]{2,1,0:T(8,128)(2,1)S(1)}, bf16[2,64,1024]{...) custom-call(s32[6]{0:T(128)S(1)} %pad_add_fusion.meta, ...), custom_call_target="tpu_custom_call" | custom-call | flops 2684354560 | bytes 4194304 | tf_op jit(solution)/shard_map/pallas_call | solution.py:27
  87.0 4.3 %collective-permute-start.9 = (bf16[2,64,1024]{2,1,0:T(8,128)(2,1)S(1)}, bf16[2,64,1024]{2,1,0:T(8,128)(2,1)S(1)}, u32[]{:S(2)}, u32[]{:S(2)}) collective-permute-start(bf16[2,64,1024]{2,1,0:T(8,128)(2,1)S(1)} %get-tuple-element.51), channel_id=1, source_target_pairs={{0,16},{1,17},{2,18},{3,19},{4,20},{5,21},{6,22},{7,23},{8,24},{9,... | collective-permute-start | bytes 786440 | tf_op jit(solution)/shard_map/ppermute | solution.py:331
  91.4 3.6 %collective-permute-start.10 = (bf16[2,64,1024]{2,1,0:T(8,128)(2,1)S(1)}, bf16[2,64,1024]{2,1,0:T(8,128)(2,1)S(1)}, u32[]{:S(2)}, u32[]{:S(2)}) collective-permute-start(bf16[2,64,1024]{2,1,0:T(8,128)(2,1)S(1)} %get-tuple-element.52), channel_id=1, source_target_pairs={{0,20},{1,21},{2,22},{3,23},{4,24},{5,25},{6,26},{7,27},{8,28},{9,... | collective-permute-start | bytes 786440 | tf_op jit(solution)/shard_map/ppermute | solution.py:331
  95.0 2.8 %collective-permute-start.11 = (bf16[2,64,1024]{2,1,0:T(8,128)(2,1)S(1)}, bf16[2,64,1024]{2,1,0:T(8,128)(2,1)S(1)}, u32[]{:S(2)}, u32[]{:S(2)}) collective-permute-start(bf16[2,64,1024]{2,1,0:T(8,128)(2,1)S(1)} %get-tuple-element.53), channel_id=1, source_target_pairs={{0,24},{1,25},{2,26},{3,27},{4,28},{5,29},{6,30},{7,31},{8,16},{9,... | collective-permute-start | bytes 786440 | tf_op jit(solution)/shard_map/ppermute | solution.py:331
  97.8 3.2 %collective-permute-start.12 = (bf16[2,64,1024]{2,1,0:T(8,128)(2,1)S(1)}, bf16[2,64,1024]{2,1,0:T(8,128)(2,1)S(1)}, u32[]{:S(2)}, u32[]{:S(2)}) collective-permute-start(bf16[2,64,1024]{2,1,0:T(8,128)(2,1)S(1)} %get-tuple-element.54), channel_id=1, source_target_pairs={{0,28},{1,29},{2,30},{3,31},{4,16},{5,17},{6,18},{7,19},{8,20},{9,... | collective-permute-start | bytes 786440 | tf_op jit(solution)/shard_map/ppermute | solution.py:331
  102.3 15.4 %shard_map.110 = (bf16[2,64,1024]{2,1,0:T(8,128)(2,1)S(1)}, bf16[2,64,1024]{2,1,0:T(8,128)(2,1)S(1)}, bf16[2,64,1024]{2,1,0:T(8,128)(2,1)S(1)}, bf16[2,64,1024]{...) custom-call(s32[6]{0:T(128)S(1)} %pad_add_fusion.meta, ...), custom_call_target="tpu_custom_call" | custom-call | flops 6710886400 | bytes 8388608 | tf_op jit(solution)/shard_map/pallas_call | solution.py:27
  119.1 9.6 %collective-permute-start.26 = (bf16[4,2,2,64,128]{4,3,2,1,0:T(8,128)(2,1)S(1)}, bf16[4,2,2,64,128]{4,3,2,1,0:T(8,128)(2,1)S(1)}, u32[]{:S(2)}, u32[]{:S(2)}) collective-permute-start(bf16[4,2,2,64,128]{4,3,2,1,0:T(8,128)(2,1)S(1)} %get-tuple-element.69), channel_id=1, source_target_pairs={{0,1},{1,0},{2,3},{3,2},{4,5},{5,4},{6,7},{7,6},{8,9},{9,8},{10,11... | collective-permute-start | bytes 786440 | tf_op jit(solution)/shard_map/ppermute | solution.py:313
  128.7 4.3 %collective-permute-start.27 = (bf16[4,2,2,64,128]{4,3,2,1,0:T(8,128)(2,1)S(1)}, bf16[4,2,2,64,128]{4,3,2,1,0:T(8,128)(2,1)S(1)}, u32[]{:S(2)}, u32[]{:S(2)}) collective-permute-start(bf16[4,2,2,64,128]{4,3,2,1,0:T(8,128)(2,1)S(1)} %get-tuple-element.70), channel_id=1, source_target_pairs={{0,2},{1,3},{2,0},{3,1},{4,6},{5,7},{6,4},{7,5},{8,10},{9,11},{10,... | collective-permute-start | bytes 786440 | tf_op jit(solution)/shard_map/ppermute | solution.py:313
  133.0 1.9 %collective-permute-start.28 = (bf16[4,2,2,64,128]{4,3,2,1,0:T(8,128)(2,1)S(1)}, bf16[4,2,2,64,128]{4,3,2,1,0:T(8,128)(2,1)S(1)}, u32[]{:S(2)}, u32[]{:S(2)}) collective-permute-start(bf16[4,2,2,64,128]{4,3,2,1,0:T(8,128)(2,1)S(1)} %get-tuple-element.71), channel_id=1, source_target_pairs={{0,3},{1,2},{2,1},{3,0},{4,7},{5,6},{6,5},{7,4},{8,11},{9,10},{10,... | collective-permute-start | bytes 786440 | tf_op jit(solution)/shard_map/ppermute | solution.py:313
  136.2 3.8 %collective-permute-done.33.b1 = bf16[2,4,64,256]{3,2,1,0:T(8,128)(2,1)S(1)} collective-permute-done((bf16[2,4,64,256]{3,2,1,0:T(8,128)(2,1)S(1)}, bf16[2,4,64,256]{3,2,1,0:T(8,128)(2,1)S(1)}, u32[]{:S(2)}, u32[]{:S(2)}) %collective-permute-start.33) | collective-permute-done | bytes 262176 | tf_op jit(solution)/shard_map/ppermute | solution.py:322
  141.3 5.4 %collective-permute-done.27.b2 = bf16[4,2,2,64,128]{4,3,2,1,0:T(8,128)(2,1)S(1)} collective-permute-done((bf16[4,2,2,64,128]{4,3,2,1,0:T(8,128)(2,1)S(1)}, bf16[4,2,2,64,128]{4,3,2,1,0:T(8,128)(2,1)S(1)}, u32[]{:S(2)}, u32[]{:S(2)}) %collective-permute-start.27) | collective-permute-done | bytes 262176 | tf_op jit(solution)/shard_map/ppermute | solution.py:313
  146.7 1.6 collective-permute-start.24
  148.4 4.6 %collective-permute-done.28.b3 = bf16[4,2,2,64,128]{4,3,2,1,0:T(8,128)(2,1)S(1)} collective-permute-done((bf16[4,2,2,64,128]{4,3,2,1,0:T(8,128)(2,1)S(1)}, bf16[4,2,2,64,128]{4,3,2,1,0:T(8,128)(2,1)S(1)}, u32[]{:S(2)}, u32[]{:S(2)}) %collective-permute-start.28) | collective-permute-done | bytes 262176 | tf_op jit(solution)/shard_map/ppermute | solution.py:313
  152.9 1.8 collective-permute-start.25
  155.4 8.0 %collective-permute-done.34.b2 = bf16[2,4,64,256]{3,2,1,0:T(8,128)(2,1)S(1)} collective-permute-done((bf16[2,4,64,256]{3,2,1,0:T(8,128)(2,1)S(1)}, bf16[2,4,64,256]{3,2,1,0:T(8,128)(2,1)S(1)}, u32[]{:S(2)}, u32[]{:S(2)}) %collective-permute-start.34) | collective-permute-done | bytes 262176 | tf_op jit(solution)/shard_map/ppermute | solution.py:322
  163.4 1.7 collective-permute-start.29
  165.1 6.1 %collective-permute-start.30 = (bf16[2,2,64,128]{3,2,1,0:T(8,128)(2,1)S(1)}, bf16[2,2,64,128]{3,2,1,0:T(8,128)(2,1)S(1)}, u32[]{:S(2)}, u32[]{:S(2)}) collective-permute-start(bf16[2,2,64,128]{3,2,1,0:T(8,128)(2,1)S(1)} %get-tuple-element.74), channel_id=1, source_target_pairs={{0,8},{1,9},{2,10},{3,11},{4,12},{5,13},{6,14},{7,15},{8,0},{9,1},... | collective-permute-start | bytes 196616 | tf_op jit(solution)/shard_map/ppermute | solution.py:309
  172.3 1.6 shard_map.106
  173.9 1.6 shard_map.114
  175.5 1.6 shard_map.111
  (72 shorter events, 28.9 us)
Async XLA Ops:
  15.6 9.4 %collective-permute-start.16 = (bf16[4,2,2,64,128]{4,3,2,1,0:T(8,128)(2,1)S(1)}, bf16[4,2,2,64,128]{4,3,2,1,0:T(8,128)(2,1)S(1)}, u32[]{:S(2)}, u32[]{:S(2)}) collective-permute-start(bf16[4,2,2,64,128]{4,3,2,1,0:T(8,128)(2,1)S(1)} %get-tuple-element.59.own), channel_id=1, source_target_pairs={{0,1},{1,0},{2,3},{3,2},{4,5},{5,4},{6,7},{7,6},{8,9},{9,8},{10,11... | collective-permute-start | bytes 786440 | tf_op jit(solution)/shard_map/ppermute | solution.py:313
  17.3 9.6 %collective-permute-start = (bf16[2,64,1024]{2,1,0:T(8,128)(2,1)S(1)}, bf16[2,64,1024]{2,1,0:T(8,128)(2,1)S(1)}, u32[]{:S(2)}, u32[]{:S(2)}) collective-permute-start(bf16[2,64,1024]{2,1,0:T(8,128)(2,1)S(1)} %get-tuple-element.43), channel_id=1, source_target_pairs={{0,4},{1,5},{2,6},{3,7},{4,8},{5,9},{6,10},{7,11},{8,12},{9,13},{1... | collective-permute-start | bytes 786440 | tf_op jit(solution)/shard_map/ppermute | solution.py:309
  18.6 13.1 %collective-permute-start.1 = (bf16[2,64,1024]{2,1,0:T(8,128)(2,1)S(1)}, bf16[2,64,1024]{2,1,0:T(8,128)(2,1)S(1)}, u32[]{:S(2)}, u32[]{:S(2)}) collective-permute-start(bf16[2,64,1024]{2,1,0:T(8,128)(2,1)S(1)} %get-tuple-element.44), channel_id=1, source_target_pairs={{0,8},{1,9},{2,10},{3,11},{4,12},{5,13},{6,14},{7,15},{8,0},{9,1},... | collective-permute-start | bytes 786440 | tf_op jit(solution)/shard_map/ppermute | solution.py:309
  21.0 12.1 %collective-permute-start.2 = (bf16[2,64,1024]{2,1,0:T(8,128)(2,1)S(1)}, bf16[2,64,1024]{2,1,0:T(8,128)(2,1)S(1)}, u32[]{:S(2)}, u32[]{:S(2)}) collective-permute-start(bf16[2,64,1024]{2,1,0:T(8,128)(2,1)S(1)} %get-tuple-element.45), channel_id=1, source_target_pairs={{0,12},{1,13},{2,14},{3,15},{4,0},{5,1},{6,2},{7,3},{8,4},{9,5},{1... | collective-permute-start | bytes 786440 | tf_op jit(solution)/shard_map/ppermute | solution.py:309
  23.2 12.9 %collective-permute-start.19 = (bf16[2,4,64,256]{3,2,1,0:T(8,128)(2,1)S(1)}, bf16[2,4,64,256]{3,2,1,0:T(8,128)(2,1)S(1)}, u32[]{:S(2)}, u32[]{:S(2)}) collective-permute-start(bf16[2,4,64,256]{3,2,1,0:T(8,128)(2,1)S(1)} %get-tuple-element.60), channel_id=1, source_target_pairs={{128,112},{129,113},{130,114},{131,115},{132,116},{133,117},{134,1... | collective-permute-start | bytes 786440 | tf_op jit(solution)/shard_map/ppermute | solution.py:322
  25.5 46.7 %collective-permute-start.17 = (bf16[2,4,2,2,64,128]{5,4,3,2,1,0:T(8,128)(2,1)S(1)}, bf16[2,4,2,2,64,128]{5,4,3,2,1,0:T(8,128)(2,1)S(1)}, u32[]{:S(2)}, u32[]{:S(2)}) collective-permute-start(bf16[2,4,2,2,64,128]{5,4,3,2,1,0:T(8,128)(2,1)S(1)} %shard_map.108.rest_4_), channel_id=1, source_target_pairs={{1,2},{2,1},{5,6},{6,5},{9,10},{10,9},{13,14},{14,13},{17,18},{18,... | collective-permute-start | bytes 1572872 | tf_op jit(solution)/shard_map/ppermute | solution.py:337
  26.9 16.2 %collective-permute-start.20 = (bf16[2,4,64,256]{3,2,1,0:T(8,128)(2,1)S(1)}, bf16[2,4,64,256]{3,2,1,0:T(8,128)(2,1)S(1)}, u32[]{:S(2)}, u32[]{:S(2)}) collective-permute-start(bf16[2,4,64,256]{3,2,1,0:T(8,128)(2,1)S(1)} %get-tuple-element.61), channel_id=1, source_target_pairs={{128,113},{129,112},{130,115},{131,114},{132,117},{133,116},{134,1... | collective-permute-start | bytes 786440 | tf_op jit(solution)/shard_map/ppermute | solution.py:322
  31.7 30.0 %collective-permute-start.21 = (bf16[2,4,64,256]{3,2,1,0:T(8,128)(2,1)S(1)}, bf16[2,4,64,256]{3,2,1,0:T(8,128)(2,1)S(1)}, u32[]{:S(2)}, u32[]{:S(2)}) collective-permute-start(bf16[2,4,64,256]{3,2,1,0:T(8,128)(2,1)S(1)} %get-tuple-element.62), channel_id=1, source_target_pairs={{128,114},{129,115},{130,112},{131,113},{132,118},{133,119},{134,1... | collective-permute-start | bytes 786440 | tf_op jit(solution)/shard_map/ppermute | solution.py:322
  33.1 30.1 %collective-permute-start.8 = (bf16[4,2,2,64,128]{4,3,2,1,0:T(8,128)(2,1)S(1)}, bf16[4,2,2,64,128]{4,3,2,1,0:T(8,128)(2,1)S(1)}, u32[]{:S(2)}, u32[]{:S(2)}) collective-permute-start(bf16[4,2,2,64,128]{4,3,2,1,0:T(8,128)(2,1)S(1)} %get-tuple-element.50.k0), channel_id=1, source_target_pairs={{0,3},{1,2},{2,1},{3,0},{4,7},{5,6},{6,5},{7,4},{8,11},{9,10},{10,... | collective-permute-start | bytes 786440 | tf_op jit(solution)/shard_map/ppermute | solution.py:313
  36.1 36.0 %collective-permute-start.7 = (bf16[4,2,2,64,128]{4,3,2,1,0:T(8,128)(2,1)S(1)}, bf16[4,2,2,64,128]{4,3,2,1,0:T(8,128)(2,1)S(1)}, u32[]{:S(2)}, u32[]{:S(2)}) collective-permute-start(bf16[4,2,2,64,128]{4,3,2,1,0:T(8,128)(2,1)S(1)} %get-tuple-element.50.k0), channel_id=1, source_target_pairs={{0,2},{1,3},{2,0},{3,1},{4,6},{5,7},{6,4},{7,5},{8,10},{9,11},{10,... | collective-permute-start | bytes 786440 | tf_op jit(solution)/shard_map/ppermute | solution.py:313
  43.1 30.6 %collective-permute-start.6 = (bf16[4,2,2,64,128]{4,3,2,1,0:T(8,128)(2,1)S(1)}, bf16[4,2,2,64,128]{4,3,2,1,0:T(8,128)(2,1)S(1)}, u32[]{:S(2)}, u32[]{:S(2)}) collective-permute-start(bf16[4,2,2,64,128]{4,3,2,1,0:T(8,128)(2,1)S(1)} %get-tuple-element.50.k0), channel_id=1, source_target_pairs={{0,1},{1,0},{2,3},{3,2},{4,5},{5,4},{6,7},{7,6},{8,9},{9,8},{10,11... | collective-permute-start | bytes 786440 | tf_op jit(solution)/shard_map/ppermute | solution.py:313
  61.8 29.6 %collective-permute-start.13 = (bf16[2,2,64,1024]{3,2,1,0:T(8,128)(2,1)S(1)}, bf16[2,2,64,1024]{3,2,1,0:T(8,128)(2,1)S(1)}, u32[]{:S(2)}, u32[]{:S(2)}) collective-permute-start(bf16[2,2,64,1024]{3,2,1,0:T(8,128)(2,1)S(1)} %get-tuple-element.56), channel_id=1, source_target_pairs={{0,4},{1,5},{2,6},{3,7},{4,8},{5,9},{6,10},{7,11},{8,12},{9,13},{1... | collective-permute-start | bytes 1572872 | tf_op jit(solution)/shard_map/ppermute | solution.py:309
  63.2 31.8 %collective-permute-start.14 = (bf16[2,2,64,1024]{3,2,1,0:T(8,128)(2,1)S(1)}, bf16[2,2,64,1024]{3,2,1,0:T(8,128)(2,1)S(1)}, u32[]{:S(2)}, u32[]{:S(2)}) collective-permute-start(bf16[2,2,64,1024]{3,2,1,0:T(8,128)(2,1)S(1)} %get-tuple-element.57), channel_id=1, source_target_pairs={{0,8},{1,9},{2,10},{3,11},{4,12},{5,13},{6,14},{7,15},{8,0},{9,1},... | collective-permute-start | bytes 1572872 | tf_op jit(solution)/shard_map/ppermute | solution.py:309
  72.1 25.7 %collective-permute-start.15 = (bf16[2,2,64,1024]{3,2,1,0:T(8,128)(2,1)S(1)}, bf16[2,2,64,1024]{3,2,1,0:T(8,128)(2,1)S(1)}, u32[]{:S(2)}, u32[]{:S(2)}) collective-permute-start(bf16[2,2,64,1024]{3,2,1,0:T(8,128)(2,1)S(1)} %get-tuple-element.58), channel_id=1, source_target_pairs={{0,12},{1,13},{2,14},{3,15},{4,0},{5,1},{6,2},{7,3},{8,4},{9,5},{1... | collective-permute-start | bytes 1572872 | tf_op jit(solution)/shard_map/ppermute | solution.py:309
  72.2 28.8 %collective-permute-start.18 = (bf16[2,4,2,2,64,128]{5,4,3,2,1,0:T(8,128)(2,1)S(1)}, bf16[2,4,2,2,64,128]{5,4,3,2,1,0:T(8,128)(2,1)S(1)}, u32[]{:S(2)}, u32[]{:S(2)}) collective-permute-start(bf16[2,4,2,2,64,128]{5,4,3,2,1,0:T(8,128)(2,1)S(1)} %collective-permute-done.17.rest_5_), channel_id=1, source_target_pairs={{1,0},{2,3},{5,4},{6,7},{9,8},{10,11},{13,12},{14,15},{17,16},{18,... | collective-permute-start | bytes 1572872 | tf_op jit(solution)/shard_map/ppermute | solution.py:339
  73.6 13.4 %collective-permute-start.22 = (bf16[2,4,64,256]{3,2,1,0:T(8,128)(2,1)S(1)}, bf16[2,4,64,256]{3,2,1,0:T(8,128)(2,1)S(1)}, u32[]{:S(2)}, u32[]{:S(2)}) collective-permute-start(bf16[2,4,64,256]{3,2,1,0:T(8,128)(2,1)S(1)} %get-tuple-element.63), channel_id=1, source_target_pairs={{128,115},{129,114},{130,113},{131,112},{132,119},{133,118},{134,1... | collective-permute-start | bytes 786440 | tf_op jit(solution)/shard_map/ppermute | solution.py:322
  87.0 30.7 %collective-permute-start.9 = (bf16[2,64,1024]{2,1,0:T(8,128)(2,1)S(1)}, bf16[2,64,1024]{2,1,0:T(8,128)(2,1)S(1)}, u32[]{:S(2)}, u32[]{:S(2)}) collective-permute-start(bf16[2,64,1024]{2,1,0:T(8,128)(2,1)S(1)} %get-tuple-element.51), channel_id=1, source_target_pairs={{0,16},{1,17},{2,18},{3,19},{4,20},{5,21},{6,22},{7,23},{8,24},{9,... | collective-permute-start | bytes 786440 | tf_op jit(solution)/shard_map/ppermute | solution.py:331
  91.4 27.7 %collective-permute-start.10 = (bf16[2,64,1024]{2,1,0:T(8,128)(2,1)S(1)}, bf16[2,64,1024]{2,1,0:T(8,128)(2,1)S(1)}, u32[]{:S(2)}, u32[]{:S(2)}) collective-permute-start(bf16[2,64,1024]{2,1,0:T(8,128)(2,1)S(1)} %get-tuple-element.52), channel_id=1, source_target_pairs={{0,20},{1,21},{2,22},{3,23},{4,24},{5,25},{6,26},{7,27},{8,28},{9,... | collective-permute-start | bytes 786440 | tf_op jit(solution)/shard_map/ppermute | solution.py:331
  95.0 33.7 %collective-permute-start.11 = (bf16[2,64,1024]{2,1,0:T(8,128)(2,1)S(1)}, bf16[2,64,1024]{2,1,0:T(8,128)(2,1)S(1)}, u32[]{:S(2)}, u32[]{:S(2)}) collective-permute-start(bf16[2,64,1024]{2,1,0:T(8,128)(2,1)S(1)} %get-tuple-element.53), channel_id=1, source_target_pairs={{0,24},{1,25},{2,26},{3,27},{4,28},{5,29},{6,30},{7,31},{8,16},{9,... | collective-permute-start | bytes 786440 | tf_op jit(solution)/shard_map/ppermute | solution.py:331
  97.8 35.2 %collective-permute-start.12 = (bf16[2,64,1024]{2,1,0:T(8,128)(2,1)S(1)}, bf16[2,64,1024]{2,1,0:T(8,128)(2,1)S(1)}, u32[]{:S(2)}, u32[]{:S(2)}) collective-permute-start(bf16[2,64,1024]{2,1,0:T(8,128)(2,1)S(1)} %get-tuple-element.54), channel_id=1, source_target_pairs={{0,28},{1,29},{2,30},{3,31},{4,16},{5,17},{6,18},{7,19},{8,20},{9,... | collective-permute-start | bytes 786440 | tf_op jit(solution)/shard_map/ppermute | solution.py:331
  101.0 33.9 %collective-permute-start.32 = (bf16[2,4,64,256]{3,2,1,0:T(8,128)(2,1)S(1)}, bf16[2,4,64,256]{3,2,1,0:T(8,128)(2,1)S(1)}, u32[]{:S(2)}, u32[]{:S(2)}) collective-permute-start(bf16[2,4,64,256]{3,2,1,0:T(8,128)(2,1)S(1)} %get-tuple-element.76), channel_id=1, source_target_pairs={{0,240},{1,241},{2,242},{3,243},{4,244},{5,245},{6,246},{7,247},{8... | collective-permute-start | bytes 786440 | tf_op jit(solution)/shard_map/ppermute | solution.py:322
  117.8 22.2 %collective-permute-start.33 = (bf16[2,4,64,256]{3,2,1,0:T(8,128)(2,1)S(1)}, bf16[2,4,64,256]{3,2,1,0:T(8,128)(2,1)S(1)}, u32[]{:S(2)}, u32[]{:S(2)}) collective-permute-start(bf16[2,4,64,256]{3,2,1,0:T(8,128)(2,1)S(1)} %get-tuple-element.77), channel_id=1, source_target_pairs={{0,241},{1,240},{2,243},{3,242},{4,245},{5,244},{6,247},{7,246},{8... | collective-permute-start | bytes 786440 | tf_op jit(solution)/shard_map/ppermute | solution.py:322
  119.1 22.2 %collective-permute-start.26 = (bf16[4,2,2,64,128]{4,3,2,1,0:T(8,128)(2,1)S(1)}, bf16[4,2,2,64,128]{4,3,2,1,0:T(8,128)(2,1)S(1)}, u32[]{:S(2)}, u32[]{:S(2)}) collective-permute-start(bf16[4,2,2,64,128]{4,3,2,1,0:T(8,128)(2,1)S(1)} %get-tuple-element.69), channel_id=1, source_target_pairs={{0,1},{1,0},{2,3},{3,2},{4,5},{5,4},{6,7},{7,6},{8,9},{9,8},{10,11... | collective-permute-start | bytes 786440 | tf_op jit(solution)/shard_map/ppermute | solution.py:313
  128.7 18.0 %collective-permute-start.27 = (bf16[4,2,2,64,128]{4,3,2,1,0:T(8,128)(2,1)S(1)}, bf16[4,2,2,64,128]{4,3,2,1,0:T(8,128)(2,1)S(1)}, u32[]{:S(2)}, u32[]{:S(2)}) collective-permute-start(bf16[4,2,2,64,128]{4,3,2,1,0:T(8,128)(2,1)S(1)} %get-tuple-element.70), channel_id=1, source_target_pairs={{0,2},{1,3},{2,0},{3,1},{4,6},{5,7},{6,4},{7,5},{8,10},{9,11},{10,... | collective-permute-start | bytes 786440 | tf_op jit(solution)/shard_map/ppermute | solution.py:313
  133.0 20.0 %collective-permute-start.28 = (bf16[4,2,2,64,128]{4,3,2,1,0:T(8,128)(2,1)S(1)}, bf16[4,2,2,64,128]{4,3,2,1,0:T(8,128)(2,1)S(1)}, u32[]{:S(2)}, u32[]{:S(2)}) collective-permute-start(bf16[4,2,2,64,128]{4,3,2,1,0:T(8,128)(2,1)S(1)} %get-tuple-element.71), channel_id=1, source_target_pairs={{0,3},{1,2},{2,1},{3,0},{4,7},{5,6},{6,5},{7,4},{8,11},{9,10},{10,... | collective-permute-start | bytes 786440 | tf_op jit(solution)/shard_map/ppermute | solution.py:313
  134.9 28.5 %collective-permute-start.34 = (bf16[2,4,64,256]{3,2,1,0:T(8,128)(2,1)S(1)}, bf16[2,4,64,256]{3,2,1,0:T(8,128)(2,1)S(1)}, u32[]{:S(2)}, u32[]{:S(2)}) collective-permute-start(bf16[2,4,64,256]{3,2,1,0:T(8,128)(2,1)S(1)} %get-tuple-element.78), channel_id=1, source_target_pairs={{0,242},{1,243},{2,240},{3,241},{4,246},{5,247},{6,244},{7,245},{8... | collective-permute-start | bytes 786440 | tf_op jit(solution)/shard_map/ppermute | solution.py:322
  139.9 25.2 %collective-permute-start.35 = (bf16[2,4,64,256]{3,2,1,0:T(8,128)(2,1)S(1)}, bf16[2,4,64,256]{3,2,1,0:T(8,128)(2,1)S(1)}, u32[]{:S(2)}, u32[]{:S(2)}) collective-permute-start(bf16[2,4,64,256]{3,2,1,0:T(8,128)(2,1)S(1)} %get-tuple-element.79), channel_id=1, source_target_pairs={{0,243},{1,242},{2,241},{3,240},{4,247},{5,246},{6,245},{7,244},{8... | collective-permute-start | bytes 786440 | tf_op jit(solution)/shard_map/ppermute | solution.py:322
  141.2 30.0 %collective-permute-start.23 = (bf16[2,64,1024]{2,1,0:T(8,128)(2,1)S(1)}, bf16[2,64,1024]{2,1,0:T(8,128)(2,1)S(1)}, u32[]{:S(2)}, u32[]{:S(2)}) collective-permute-start(bf16[2,64,1024]{2,1,0:T(8,128)(2,1)S(1)} %get-tuple-element.65), channel_id=1, source_target_pairs={{0,4},{1,5},{2,6},{3,7},{4,8},{5,9},{6,10},{7,11},{8,12},{9,13},{1... | collective-permute-start | bytes 786440 | tf_op jit(solution)/shard_map/ppermute | solution.py:309
  146.7 28.8 %collective-permute-start.24 = (bf16[2,64,1024]{2,1,0:T(8,128)(2,1)S(1)}, bf16[2,64,1024]{2,1,0:T(8,128)(2,1)S(1)}, u32[]{:S(2)}, u32[]{:S(2)}) collective-permute-start(bf16[2,64,1024]{2,1,0:T(8,128)(2,1)S(1)} %get-tuple-element.66), channel_id=1, source_target_pairs={{0,8},{1,9},{2,10},{3,11},{4,12},{5,13},{6,14},{7,15},{8,0},{9,1},... | collective-permute-start | bytes 786440 | tf_op jit(solution)/shard_map/ppermute | solution.py:309
  152.9 22.5 %collective-permute-start.25 = (bf16[2,64,1024]{2,1,0:T(8,128)(2,1)S(1)}, bf16[2,64,1024]{2,1,0:T(8,128)(2,1)S(1)}, u32[]{:S(2)}, u32[]{:S(2)}) collective-permute-start(bf16[2,64,1024]{2,1,0:T(8,128)(2,1)S(1)} %get-tuple-element.67), channel_id=1, source_target_pairs={{0,12},{1,13},{2,14},{3,15},{4,0},{5,1},{6,2},{7,3},{8,4},{9,5},{1... | collective-permute-start | bytes 786440 | tf_op jit(solution)/shard_map/ppermute | solution.py:309
  163.4 13.7 %collective-permute-start.29 = (bf16[2,2,64,128]{3,2,1,0:T(8,128)(2,1)S(1)}, bf16[2,2,64,128]{3,2,1,0:T(8,128)(2,1)S(1)}, u32[]{:S(2)}, u32[]{:S(2)}) collective-permute-start(bf16[2,2,64,128]{3,2,1,0:T(8,128)(2,1)S(1)} %get-tuple-element.73), channel_id=1, source_target_pairs={{0,4},{1,5},{2,6},{3,7},{4,8},{5,9},{6,10},{7,11},{8,12},{9,13},{1... | collective-permute-start | bytes 196616 | tf_op jit(solution)/shard_map/ppermute | solution.py:309
  165.1 12.0 %collective-permute-start.30 = (bf16[2,2,64,128]{3,2,1,0:T(8,128)(2,1)S(1)}, bf16[2,2,64,128]{3,2,1,0:T(8,128)(2,1)S(1)}, u32[]{:S(2)}, u32[]{:S(2)}) collective-permute-start(bf16[2,2,64,128]{3,2,1,0:T(8,128)(2,1)S(1)} %get-tuple-element.74), channel_id=1, source_target_pairs={{0,8},{1,9},{2,10},{3,11},{4,12},{5,13},{6,14},{7,15},{8,0},{9,1},... | collective-permute-start | bytes 196616 | tf_op jit(solution)/shard_map/ppermute | solution.py:309
  (12 other events, 157.3 us)
